TPU v7x, 128 devices: a whole 4x4x4 slice. The times are simulated.
128 devices in a mesh: seq: 16 (over y, x_lo, core), tensor: 8 (over z, x_hi).
Axes of the slice: x: 4 (x_hi: 2, x_lo: 2; x = x_hi * 2 + x_lo), y: 4, z: 4, core: 2. Of those that a mesh axis runs over, the one named last changes fastest.
Arguments:
- audio_codes: int32 [4096, 8], P('seq'), may hold values from 0 to 1023
- chroma_ids: int32 [4096], P('seq'), may hold values from 0 to 255
- song_ids: int32 [4096], P('seq'), may hold values from 0 to 3, never falling along the last dimension, each value on 1 to 2048 neighbouring positions
- code_table: bfloat16 [8, 1024, 4096], P(None, 'seq', 'tensor'), may hold values from -2.5 to 2.5
- chroma_table: bfloat16 [256, 4096], P(None, 'tensor'), may hold values from -2.5 to 2.5
- attention_gain: float32 [4096], replicated, may hold values from 0.1 to 1.9
- temporal_qkv: bfloat16 [3, 4096, 4096], P(None, None, 'tensor'), may hold values from -0.390625 to 0.390625
- temporal_out: bfloat16 [4096, 4096], P('tensor'), may hold values from -0.375 to 0.375
- output_gain: float32 [4096], replicated, may hold values from 0.1 to 1.9
- depth_input: bfloat16 [4096, 1024], P(None, 'tensor'), may hold values from -0.09375 to 0.09375
- depth_table: bfloat16 [7, 1024, 1024], P(None, None, 'tensor'), may hold values from -3 to 3
- depth_gain: float32 [1024], replicated, may hold values from 0.1 to 1.9
- depth_qkv: bfloat16 [3, 1024, 1024], P(None, None, 'tensor'), may hold values from -1.65625 to 1.65625
- depth_proj: bfloat16 [1024, 1024], P('tensor'), may hold values from -0.5 to 0.5
Outputs:
- temporal_hidden: bfloat16 [4096, 4096], P(('seq', 'tensor'))
- depth_hidden: bfloat16 [4096, 8, 1024], P(('seq', 'tensor'))
All inputs are finite; a program needn't handle non-finite values.
Results may differ from a plain program's by a relative error of at most 0.029.
Values may be sent and summed in bfloat16 or wider, within the bound.
A program may use at most 192 MiB of HBM per device.

v0:
```python
import jax
import jax.numpy as jnp
from jax import lax
from jax.sharding import PartitionSpec as P

HEAD = 128
DHEAD = 64
BOOKS = 8


def rms_norm(entries, norm_gain):
    entries = entries.astype(jnp.float32)
    factor = lax.rsqrt(jnp.mean(entries * entries, axis=-1, keepdims=True) + 1e-05)
    return (entries * factor * norm_gain).astype(jnp.bfloat16)


def rotate(entries, positions):
    half_width = entries.shape[-1] // 2
    frequencies = 10000.0 ** (
        -(jnp.arange(half_width, dtype=jnp.float32) * 2.0 / entries.shape[-1])
    )
    angles = positions.astype(jnp.float32)[:, None] * frequencies[None, :]
    cosines = jnp.cos(angles)[:, None, :]
    sines = jnp.sin(angles)[:, None, :]
    leading = entries[..., :half_width]
    trailing = entries[..., half_width:]
    return jnp.concatenate(
        [leading * cosines - trailing * sines, leading * sines + trailing * cosines], axis=-1
    )


def depth_attend(queries, keys_here, values_here):
    codebooks = queries.shape[1]
    scores = jnp.einsum(
        "fqhd,fkhd->fhqk", queries, keys_here, preferred_element_type=jnp.float32
    ) * queries.shape[3] ** (-0.5)
    ranks = jnp.arange(codebooks, dtype=jnp.int32)
    allowed = ranks[:, None] >= ranks[None, :]
    highest = jnp.max(jnp.where(allowed, scores, -1e30), axis=3, keepdims=True)
    weights = jnp.where(allowed, jnp.exp(scores - highest), 0.0)
    totals = jnp.sum(weights, axis=3, keepdims=True)
    blended = (
        jnp.einsum(
            "fhqk,fkhd->fhqd",
            weights.astype(jnp.bfloat16),
            values_here,
            preferred_element_type=jnp.float32,
        )
        / totals
    )
    frames_here = queries.shape[0]
    return blended.transpose(0, 2, 1, 3).reshape(frames_here * codebooks, -1).astype(jnp.bfloat16)


def look_up(tables, identifiers):
    entry_count = tables.shape[1]
    offsets = identifiers
    inside = (offsets >= 0) & (offsets < entry_count)
    offsets = jnp.clip(offsets, 0, entry_count - 1)
    summed = jnp.zeros((identifiers.shape[0], tables.shape[2]), jnp.float32)
    for codebook in range(BOOKS):
        picked = jnp.take(tables[codebook], offsets[:, codebook], axis=0).astype(jnp.float32)
        summed = summed + jnp.where(inside[:, codebook, None], picked, 0.0)
    return summed


def depth_projections(depth_normed, weights_qkv, frames_here, codebooks):
    projected_parts = []
    for which in range(3):
        part_here = jnp.dot(
            depth_normed, weights_qkv[which], preferred_element_type=jnp.float32
        ).astype(jnp.bfloat16)
        projected_parts.append(part_here.reshape(frames_here, codebooks, -1, DHEAD))
    return projected_parts


def shards(
    audio_codes,
    chroma_ids,
    song_ids,
    code_table,
    chroma_table,
    attention_gain,
    temporal_qkv,
    temporal_out,
    output_gain,
    depth_input,
    depth_table,
    depth_gain,
    depth_qkv,
    depth_proj,
):
    frame_count = audio_codes.shape[0]
    codebooks = audio_codes.shape[1]
    tensor_rank = lax.axis_index("tensor")
    own_frames = frame_count // lax.axis_size("tensor")
    local_width = temporal_qkv.shape[2]
    local_heads = local_width // HEAD
    embedded = look_up(lax.all_gather(code_table, "seq", axis=1, tiled=True), audio_codes)
    chroma_onehot = (
        chroma_ids[:, None] == jnp.arange(chroma_table.shape[0], dtype=jnp.int32)[None, :]
    ).astype(jnp.bfloat16)
    tokens_local = (
        embedded + jnp.dot(chroma_onehot, chroma_table, preferred_element_type=jnp.float32)
    ).astype(jnp.bfloat16)
    depth_columns = jnp.stack(
        [
            jnp.take(depth_table[codebook], audio_codes[:, codebook], axis=0)
            for codebook in range(BOOKS - 1)
        ],
        axis=1,
    )
    tokens, depth_lookups = (
        lax.all_gather(tokens_local, "tensor", axis=1, tiled=True),
        lax.all_gather(depth_columns, "tensor", axis=2, tiled=True),
    )
    normed = rms_norm(tokens, attention_gain)
    positions = lax.axis_index("seq") * frame_count + jnp.arange(frame_count, dtype=jnp.int32)
    queries = rotate(
        jnp.dot(normed, temporal_qkv[0], preferred_element_type=jnp.float32).reshape(
            frame_count, local_heads, HEAD
        ),
        positions,
    ).astype(jnp.bfloat16)
    keys_local = (
        rotate(
            jnp.dot(normed, temporal_qkv[1], preferred_element_type=jnp.float32).reshape(
                frame_count, local_heads, HEAD
            ),
            positions,
        )
        .astype(jnp.bfloat16)
        .reshape(frame_count, local_width)
    )
    values_local = jnp.dot(normed, temporal_qkv[2], preferred_element_type=jnp.float32).astype(
        jnp.bfloat16
    )
    score_scale = HEAD ** (-0.5)
    last_query = positions[frame_count - 1]
    starting = (
        jnp.full((frame_count, local_heads), -1e30, jnp.float32),
        jnp.zeros((frame_count, local_heads), jnp.float32),
        jnp.zeros((frame_count, local_heads, HEAD), jnp.float32),
    )
    block_keys = lax.all_gather(keys_local, "seq", axis=0, tiled=True)
    block_values = lax.all_gather(values_local, "seq", axis=0, tiled=True)
    block_songs = lax.all_gather(song_ids, "seq", axis=0, tiled=True)
    block_count = block_keys.shape[0]

    def update(current):
        highest, totals, accumulated = current
        key_positions = jnp.arange(block_count, dtype=jnp.int32)
        allowed = (song_ids[:, None] == block_songs[None, :]) & (
            positions[:, None] >= key_positions[None, :]
        )
        allowed = allowed[:, None, :]
        scores = (
            jnp.einsum(
                "qhd,khd->qhk",
                queries,
                block_keys.reshape(block_count, local_heads, HEAD),
                preferred_element_type=jnp.float32,
            )
            * score_scale
        )
        block_high = jnp.max(jnp.where(allowed, scores, -1e30), axis=2)
        new_high = jnp.maximum(highest, block_high)
        weights = jnp.where(allowed, jnp.exp(scores - new_high[:, :, None]), 0.0)
        totals = jnp.sum(weights, axis=2)
        accumulated = jnp.einsum(
            "qhk,khd->qhd",
            weights.astype(jnp.bfloat16),
            block_values.reshape(block_count, local_heads, HEAD),
            preferred_element_type=jnp.float32,
        )
        return (new_high, totals, accumulated)

    highest, totals, accumulated = lax.cond(
        jnp.int32(0) <= last_query, update, lambda unchanged: unchanged, starting
    )
    attended = (
        (accumulated / totals[:, :, None]).astype(jnp.bfloat16).reshape(frame_count, local_width)
    )
    frame_start = tensor_rank * own_frames
    own_tokens = lax.dynamic_slice_in_dim(tokens, frame_start, own_frames, 0).astype(jnp.float32)
    temporal_hidden = (
        own_tokens
        + lax.psum_scatter(
            jnp.dot(attended, temporal_out, preferred_element_type=jnp.float32),
            "tensor",
            scatter_dimension=0,
            tiled=True,
        )
    ).astype(jnp.bfloat16)
    normed_hidden = rms_norm(temporal_hidden, output_gain)
    full_input, full_qkv, full_proj = (
        lax.all_gather(depth_input, "tensor", axis=1, tiled=True),
        lax.all_gather(depth_qkv, "tensor", axis=2, tiled=True),
        lax.all_gather(depth_proj, "tensor", axis=0, tiled=True),
    )
    projected = jnp.dot(normed_hidden, full_input, preferred_element_type=jnp.float32)
    lookups = lax.dynamic_slice_in_dim(depth_lookups, frame_start, own_frames, 0).astype(
        jnp.float32
    )
    depth_inputs = jnp.concatenate(
        [projected[:, None], projected[:, None] + lookups], axis=1
    ).astype(jnp.bfloat16)
    flattened = depth_inputs.reshape(own_frames * codebooks, -1)
    depth_normed = rms_norm(flattened, depth_gain)
    depth_queries, depth_keys, depth_values = depth_projections(
        depth_normed, full_qkv, own_frames, codebooks
    )
    depth_mixed = depth_attend(depth_queries, depth_keys, depth_values)
    depth_hidden = (
        flattened.astype(jnp.float32)
        + jnp.dot(depth_mixed, full_proj, preferred_element_type=jnp.float32)
    ).astype(jnp.bfloat16)
    return (temporal_hidden, depth_hidden.reshape(own_frames, codebooks, -1))


def solution(mesh):
    placed = (
        P("seq", None),
        P("seq"),
        P("seq"),
        P(None, "seq", "tensor"),
        P(None, "tensor"),
        P(),
        P(None, None, "tensor"),
        P("tensor", None),
        P(),
        P(None, "tensor"),
        P(None, None, "tensor"),
        P(),
        P(None, None, "tensor"),
        P("tensor", None),
    )
    return jax.shard_map(
        shards,
        mesh=mesh,
        in_specs=placed,
        out_specs=(P(("seq", "tensor"), None), P(("seq", "tensor"), None, None)),
        check_vma=False,
    )
```

profile of v0, /device:TPU:1, one launch (start us, length us, event | category | flops | bytes accessed | tf_op | source)
XLA Modules:
  0.0 686.3 jit_solution(8260865353101435583)
XLA Ops:
  9.6 55.8 %all-gather.10.cloned.1.call-done = bf16[8,1024,512]{2,1,0:T(8,128)(2,1)} async-done(((bf16[8,64,512]{2,1,0:T(8,128)(2,1)}), bf16[8,1024,512]{2,1,0:T(8,128)(2,1)}) %all-gather.10.cloned.1.call-update) | async-done | bytes 8388624 | tf_op jit(solution)/shard_map/all_gather | solution.py:99
  65.4 5.7 slice_bitcast_fusion.21
  92.4 3.8 fusion.47
  96.4 5.8 slice_bitcast_fusion
  102.2 6.5 copy.81
  108.7 6.5 copy.79
  115.5 35.6 %all-gather.12.cloned.1.call-done = bf16[256,4096]{1,0:T(8,128)(2,1)} async-done(((bf16[256,512]{1,0:T(8,128)(2,1)}), bf16[256,4096]{1,0:T(8,128)(2,1)}) %all-gather.12.cloned.1.call-update) | async-done | bytes 2097168 | tf_op jit(solution)/shard_map/all_gather | solution.py:114
  153.2 4.3 fusion.32
  160.4 4.2 fusion.44
  166.0 19.6 %all-gather = s32[16,1,256]{2,1,0:T(1,128)S(1)} all-gather(s32[1,1,256]{2,1,0:T(1,128)S(1)} %bitcast.203), channel_id=1, replica_groups=mesh['seq'=16,'tensor'=8] {'seq'}, dimensions={0}, use_global_device_ids=true | all-gather | bytes 17408 | tf_op jit(solution)/shard_map/all_gather | solution.py:147
  185.6 10.8 %all-gather.14.cloned.1.call-done = bf16[4096,512]{1,0:T(8,128)(2,1)} async-done(((bf16[256,512]{1,0:T(8,128)(2,1)}), bf16[4096,512]{1,0:T(8,128)(2,1)}) %all-gather.14.cloned.1.call-update) | async-done | bytes 4194320 | tf_op jit(solution)/shard_map/all_gather | solution.py:145
  196.4 39.6 %all-gather.16.cloned.1.call-done = bf16[4096,512]{1,0:T(8,128)(2,1)} async-done(((bf16[256,512]{1,0:T(8,128)(2,1)}), bf16[4096,512]{1,0:T(8,128)(2,1)}) %all-gather.16.cloned.1.call-update) | async-done | bytes 4194320 | tf_op jit(solution)/shard_map/all_gather | solution.py:146
  236.0 17.8 %conditional.1 = (f32[256,4]{0,1:T(4,128)S(1)}, f32[256,4,128]{0,2,1:T(8,128)S(1)}) conditional(s32[]{:T(128)} %bitcast.18, () %tuple.18, (s32[256]{0:T(256)S(1)}, s32[4096]{0:T(1024)S(1)}, s32[256]{0:T(256)S(1)}, bf16[4096,512]{1,0:T(8,128)(2,1)}, bf16[256,4,128]{0,2,1:T(8,128)(2,1)S(1)}, /*index=5*/bf16[4096,512]{1,0:T(8,128)(2,1)}) %tuple.104), branch_computations={%region_1.3_spmd, %region_2.6_spmd} | conditional | flops 2196765696 | bytes 64792592 | solution.py:178
  237.9 4.6 fusion
  242.5 3.6 fusion.4
  246.1 7.5 %fusion.14 = f32[256,4,128]{2,0,1:T(8,128)S(1)} fusion(f32[4,4096,256]{2,1,0:T(8,128)S(1)} %get-tuple-element.68, f32[256,4]{0,1:T(4,128)S(1)} %broadcast_maximum_fusion, pred[256,4096]{0,1:T(8,128)(4,1)S(1)} %fusion.13, bf16[4096,512]{1,0:T(8,128)(2,1)} %get-tuple-element.19), kind=kOutput, calls=%fused_computation.31 | convolution fusion | flops 1090519040 | bytes 22548480 | tf_op jit(solution)/shard_map/cond/branch_1_fun/qhk,khd->qhd/dot_general | solution.py:170
  253.9 5.4 fusion.81
  270.9 71.9 %reduce-scatter.2.cloned.1.call-done = f32[32,4096]{1,0:T(8,128)} async-done(((f32[256,4096]{1,0:T(8,128)}), f32[32,4096]{1,0:T(8,128)}) %reduce-scatter.2.cloned.1.call-update) | async-done | bytes 524304 | tf_op jit(solution)/shard_map/reduce_scatter | solution.py:188
  344.2 113.8 %all-gather.18.cloned.1.call-done = bf16[4096,1024]{1,0:T(8,128)(2,1)} async-done(((bf16[4096,128]{1,0:T(8,128)(2,1)}), bf16[4096,1024]{1,0:T(8,128)(2,1)}) %all-gather.18.cloned.1.call-update) | async-done | bytes 8388624 | tf_op jit(solution)/shard_map/all_gather | solution.py:197
  458.0 5.0 fusion.64
  463.0 64.7 %all-gather.20.cloned.1.call-done = bf16[256,7,1024]{2,0,1:T(8,128)(2,1)} async-done(((bf16[256,7,128]{2,0,1:T(8,128)(2,1)}), bf16[256,7,1024]{2,0,1:T(8,128)(2,1)}) %all-gather.20.cloned.1.call-update) | async-done | bytes 3670032 | tf_op jit(solution)/shard_map/all_gather | solution.py:115
  529.2 92.3 %all-gather.22.cloned.1.call-done = bf16[3,1024,1024]{2,1,0:T(8,128)(2,1)} async-done(((bf16[3,1024,128]{2,1,0:T(8,128)(2,1)}), bf16[3,1024,1024]{2,1,0:T(8,128)(2,1)}) %all-gather.22.cloned.1.call-update) | async-done | bytes 6291472 | tf_op jit(solution)/shard_map/all_gather | solution.py:198
  640.8 35.4 %all-gather.24.cloned.1.call-done = bf16[1024,1024]{1,0:T(8,128)(2,1)} async-done(((bf16[128,1024]{1,0:T(8,128)(2,1)}), bf16[1024,1024]{1,0:T(8,128)(2,1)}) %all-gather.24.cloned.1.call-update) | async-done | bytes 2097168 | tf_op jit(solution)/shard_map/all_gather | solution.py:199
  676.2 3.5 fusion.40
  (152 shorter events, 65.1 us)
Async XLA Ops:
  7.2 85.2 %copy-start = (bf16[256,512]{1,0:T(8,128)(2,1)S(1)}, bf16[256,512]{1,0:T(8,128)(2,1)}, u32[]{:S(2)}) copy-start(bf16[256,512]{1,0:T(8,128)(2,1)} %param.24) | copy-start | bytes 786436
  7.2 58.3 %all-gather.10.cloned.1.call-start = ((), (), s32[]{:S(2)}) async-start(), calls=%async_computation.1 | async-start | bytes 8912896 | tf_op jit(solution)/shard_map/all_gather | solution.py:99
  7.9 143.2 %all-gather.12.cloned.1.call-start = ((), (), s32[]{:S(2)}) async-start(), calls=%async_computation.2 | async-start | bytes 2359296 | tf_op jit(solution)/shard_map/all_gather | solution.py:114
  84.2 8.2 %copy-start.16 = (s32[256]{0:T(256)S(1)}, s32[256]{0:T(256)}, u32[]{:S(2)}) copy-start(s32[256]{0:T(256)} %param.21) | copy-start | bytes 3076
  89.3 3.1 copy-start.7
  89.3 3.1 copy-start.8
  89.3 3.1 copy-start.9
  89.3 3.1 copy-start.10
  96.2 100.2 %all-gather.14.cloned.1.call-start = ((), (), s32[]{:S(2)}) async-start(), calls=%async_computation.3 | async-start | bytes 4456448 | tf_op jit(solution)/shard_map/all_gather | solution.py:145
  108.7 44.5 %copy-start.15 = (f32[4096]{0:T(1024)S(1)}, f32[4096]{0:T(1024)}, u32[]{:S(2)}) copy-start(f32[4096]{0:T(1024)} %param.25) | copy-start | bytes 49156
  153.2 4.4 copy-start.2
  153.2 4.7 copy-start.3
  160.3 5.6 copy-start.14
  160.3 75.7 %all-gather.16.cloned.1.call-start = ((), (), s32[]{:S(2)}) async-start(), calls=%async_computation.4 | async-start | bytes 4456448 | tf_op jit(solution)/shard_map/all_gather | solution.py:146
  164.6 178.2 %reduce-scatter.2.cloned.1.call-start = ((), (), s32[]{:S(2)}) async-start(), calls=%async_computation.5 | async-start | bytes 4718592 | tf_op jit(solution)/shard_map/reduce_scatter | solution.py:188
  259.4 198.7 %all-gather.18.cloned.1.call-start = ((), (), s32[]{:S(2)}) async-start(), calls=%async_computation.6 | async-start | bytes 9437184 | tf_op jit(solution)/shard_map/all_gather | solution.py:197
  259.9 267.8 %all-gather.20.cloned.1.call-start = ((), (), s32[]{:S(2)}) async-start(), calls=%async_computation.7 | async-start | bytes 4128768 | tf_op jit(solution)/shard_map/all_gather | solution.py:115
  261.6 196.4 %copy-start.12 = (f32[4096]{0:T(1024)S(1)}, f32[4096]{0:T(1024)}, u32[]{:S(2)}) copy-start(f32[4096]{0:T(1024)} %param.28) | copy-start | bytes 49156
  269.4 352.2 %all-gather.22.cloned.1.call-start = ((), (), s32[]{:S(2)}) async-start(), calls=%async_computation.8 | async-start | bytes 7077888 | tf_op jit(solution)/shard_map/all_gather | solution.py:198
  270.2 406.0 %all-gather.24.cloned.1.call-start = ((), (), s32[]{:S(2)}) async-start(), calls=%async_computation.9 | async-start | bytes 2359296 | tf_op jit(solution)/shard_map/all_gather | solution.py:199
  344.1 118.9 %copy-start.4 = (bf16[32,4096]{1,0:T(8,128)(2,1)}, bf16[32,4096]{1,0:T(8,128)(2,1)S(1)}, u32[]{:S(2)}) copy-start(bf16[32,4096]{1,0:T(8,128)(2,1)S(1)} %get-tuple-element.66) | copy-start | bytes 786436
  458.0 71.0 %copy-start.13 = (f32[1024]{0:T(1024)S(1)}, f32[1024]{0:T(1024)}, u32[]{:S(2)}) copy-start(f32[1024]{0:T(1024)} %param.31) | copy-start | bytes 12292
  529.2 98.8 %copy-start.6 = (bf16[32,8,1024]{2,0,1:T(8,128)(2,1)}, bf16[32,8,1024]{2,0,1:T(8,128)(2,1)S(1)}, u32[]{:S(2)}) copy-start(bf16[32,8,1024]{2,0,1:T(8,128)(2,1)S(1)} %multiply_convert_fusion) | copy-start | bytes 1572868
  639.7 40.0 %copy-start.1 = (bf16[256,512]{1,0:T(8,128)(2,1)S(1)}, bf16[256,512]{1,0:T(8,128)(2,1)}, u32[]{:S(2)}) copy-start(bf16[256,512]{1,0:T(8,128)(2,1)} %param.24) | copy-start | bytes 786436
  (2 other events, 1.5 us)
Sparse Core Ops, SparseCore 0:
  9.7 55.7 all-gather.9
  96.3 54.7 all-gather.11
  160.5 35.9 all-gather.13
  198.5 37.4 all-gather.15
  259.5 83.3 reduce-scatter.1
  345.1 112.8 all-gather.17
  461.0 66.6 all-gather.19
  530.1 91.3 all-gather.21
  624.2 51.9 all-gather.23
where the time goes:
time: 687 us; the launch traced here: 686 us
  waiting for transfers between devices  522 us (76%)
  local copies, waits for them, and re-layouts  64.1 us (9%)
  matrix products  50.3 us (7%)
  blocking collectives  19.6 us (3%)
  between operations  15.1 us (2%)
  other arithmetic  13.9 us (2%)
    all_gather x1, waiting for transfers between devices, shards(): lax.all_gather(depth_input, 'tensor', axis=1, tiled=True)  114 us
    all_gather x1, waiting for transfers between devices, shards(): lax.all_gather(depth_qkv, 'tensor', axis=2, tiled=True)  92.3 us
    reduce_scatter x1, waiting for transfers between devices, shards(): lax.psum_scatter(jnp.dot(attended, temporal_out, preferred_element_type=j...  71.9 us
    all_gather x1, waiting for transfers between devices, shards(): lax.all_gather(depth_columns, 'tensor', axis=2, tiled=True)  64.7 us
    all_gather x1, waiting for transfers between devices, shards(): lax.all_gather(code_table, 'seq', axis=1, tiled=True)  55.8 us
    all_gather x1, waiting for transfers between devices, shards(): block_values = lax.all_gather(values_local, 'seq', axis=0, tiled=True)  39.6 us
    all_gather x1, waiting for transfers between devices, shards(): lax.all_gather(tokens_local, 'tensor', axis=1, tiled=True)  35.6 us
    all_gather x1, waiting for transfers between devices, shards(): lax.all_gather(depth_proj, 'tensor', axis=0, tiled=True)  35.4 us
  transfers between devices with their start and end apart: 9, of which 9 were waited for; matrix products, arithmetic and copies ran while one was open for 9% of the time, Pallas kernels for 0%

commit v1 on v0

v1 whole, which is shorter than its diff:
```python
import functools

import jax
import jax.numpy as jnp
import numpy as np
from jax import lax
from jax.experimental import pallas as pl
from jax.experimental.pallas import tpu as pltpu
from jax.sharding import PartitionSpec as P

MESH = pl.DeviceIdType.MESH
F32 = jnp.float32
BF16 = jnp.bfloat16
HEAD = 128
DHEAD = 64
FR = 256
OWN = 32
PIECE = 2 * FR + 16


def rotation_tables():
    freq = 10000.0 ** (-(np.arange(64, dtype=np.float64) * 2.0 / HEAD))
    row = np.arange(FR, dtype=np.float64)[:, None] * freq[None]
    base = np.arange(16, dtype=np.float64)[:, None] * FR * freq[None]
    wide = lambda entries: np.concatenate([entries, entries], axis=1)
    rows = np.stack([wide(np.cos(row)), wide(np.sin(row))])
    bases = np.stack([wide(np.cos(base)), wide(np.sin(base))])
    return rows.astype(np.float32), bases.astype(np.float32)


def dot(a, b):
    return jnp.dot(a, b, preferred_element_type=F32)


def iota(shape, axis):
    return lax.broadcasted_iota(jnp.int32, shape, axis)


def kernel(
    pack_ref,
    gains_ref,
    rows_ref,
    bases_ref,
    ctab_ref,
    chroma_ref,
    wqkv_ref,
    wout_ref,
    din_ref,
    dtab_ref,
    dqkv_ref,
    dproj_ref,
    th_out,
    dh_out,
    wv,
    tab,
    hot,
    chroma,
    dtab,
    lk,
    lkf,
    cpb,
    colt,
    emb,
    psend,
    prec,
    toks,
    acc,
    kvs,
    kvb,
    qs,
    qb,
    sbuf,
    ob,
    att,
    rsend,
    rrec,
    thl,
    thb,
    di,
    pfull,
    prb,
    dq,
    dp,
    mixed,
    lsem,
    ysend,
    yrecv,
    rowsend,
    rowrecv,
    tsend,
    trecv,
):
    s = lax.axis_index("seq")
    t = lax.axis_index("tensor")
    y = s // 4
    x = (s // 2) % 2
    c = s % 2
    q4 = s % 4

    def ypeer(k):
        return (lax.rem(y + k, 4) * 4 + q4, t)

    sib = (y * 4 + x * 2 + (1 - c), t)
    xpeer = (y * 4 + (1 - x) * 2 + c, t)

    def tpeer(k):
        return (s, lax.rem(t + k, 8))

    def blk(k):
        return lax.rem(t + k, 8)

    def ring(r):
        return 2 * lax.rem(x + r // 2, 2) + lax.rem(c + r % 2, 2)

    counts = {"l": 0, "y": 0, "r": 0, "t": 0}
    pending = []

    def local(src, dst):
        n = counts["l"]
        counts["l"] += 1
        copy = pltpu.make_async_copy(src, dst, lsem.at[n])
        copy.start()
        return copy

    def remote(kind, src, dst, device):
        sends, recvs = {
            "y": (ysend, yrecv),
            "r": (rowsend, rowrecv),
            "t": (tsend, trecv),
        }[kind]
        n = counts[kind]
        counts[kind] += 1
        copy = pltpu.make_async_remote_copy(
            src_ref=src,
            dst_ref=dst,
            send_sem=sends.at[n],
            recv_sem=recvs.at[n],
            device_id=device,
            device_id_type=MESH,
        )
        copy.start()
        pending.append(copy)
        return copy

    load_dtab = local(dtab_ref, dtab)
    load_tab = local(ctab_ref, tab.at[:, 0])
    load_chroma = local(chroma_ref, chroma)
    load_w = local(wqkv_ref, wv)
    half = pl.ds(pl.multiple_of(512 * c, 512), 512)
    own_cols = pl.ds(pl.multiple_of(128 * t, 128), 128)
    load_dq = local(dqkv_ref.at[:, half], dq.at[:, half, own_cols])
    load_dp = local(
        dproj_ref.at[pl.ds(pl.multiple_of(64 * c, 64), 64)],
        dp.at[t, c],
    )
    di_half = pl.ds(pl.multiple_of(256 * c, 256), 256)
    load_di = local(
        din_ref.at[pl.ds(pl.multiple_of(512 * t + 256 * c, 256), 256)],
        di.at[di_half, own_cols],
    )

    barrier = pltpu.get_barrier_semaphore()
    greeted = [ypeer(k) for k in (1, 2, 3)] + [sib, xpeer] + [tpeer(k) for k in range(1, 8)]
    for device in greeted:
        pl.semaphore_signal(barrier, inc=1, device_id=device, device_id_type=MESH)
    pl.semaphore_wait(barrier, len(greeted))

    cpb[0] = pack_ref[...]
    code_copies = {k: remote("y", pack_ref, cpb.at[k], ypeer(k)) for k in (1, 2, 3)}
    chunk = lambda j: pl.ds(256 * j, 256)
    tab_x = [
        remote("r", ctab_ref.at[:, :, chunk(j)], tab.at[:, 2, :, chunk(j)], xpeer) for j in (0, 1)
    ]
    tab_s = [
        remote("r", ctab_ref.at[:, :, chunk(j)], tab.at[:, 1, :, chunk(j)], sib) for j in (0, 1)
    ]

    def send_di(k):
        return remote(
            "t",
            din_ref.at[pl.ds(pl.multiple_of(512 * blk(k) + 256 * c, 256), 256)],
            di.at[di_half, own_cols],
            tpeer(k),
        )

    def send_dq(i, k):
        return remote("t", dqkv_ref.at[i, half], dq.at[i, half, own_cols], tpeer(k))

    di_copies = [send_di(k) for k in range(1, 8)]
    dq_copies = {0: [send_dq(0, k) for k in range(1, 8)]}

    cpb_own = pack_ref[...].astype(F32)
    own_cols_t = jnp.transpose(cpb_own)
    colt[0] = own_cols_t
    load_dtab.wait()
    entry = iota((1, 1024), 1).astype(F32)
    for b in range(7):
        onehot = jnp.where(colt[0, :, b : b + 1] == entry, 1.0, 0.0).astype(BF16)
        lk[b] = dot(onehot, dtab[b]).astype(BF16)
    lk_copies = [
        remote(
            "t",
            lk.at[:, pl.ds(pl.multiple_of(OWN * blk(k), OWN), OWN)],
            lkf.at[:, :, own_cols],
            tpeer(k),
        )
        for k in range(1, 8)
    ]
    lkf[:, :, own_cols] = lk[:, pl.ds(pl.multiple_of(OWN * t, OWN), OWN)]

    lane = iota((1, 256), 1)
    lane_q = 2 * lax.rem(x + lane // 128, 2) + lax.rem(c + (lane // 64) % 2, 2)
    entry_row = (256 * y + 64 * lane_q + lane % 64).astype(F32)
    for k in (0, 1, 3, 2):
        if k:
            code_copies[k].wait_recv()
            colt[k] = jnp.transpose(cpb[k].astype(F32))
        for b in range(8):
            hot[k, :, 256 * b : 256 * (b + 1)] = jnp.where(
                colt[k, :, b : b + 1] == entry_row, 1.0, 0.0
            ).astype(BF16)
    load_tab.wait()

    part_copies = {}
    forwards = []
    for j in (0, 1):
        tab_x[j].wait_recv()
        forward = remote("r", tab.at[:, 2, :, chunk(j)], tab.at[:, 3, :, chunk(j)], sib)
        tab_s[j].wait_recv()
        forward.wait_recv()
        table = tab[:, :, :, 256 * j : 256 * (j + 1)].reshape(2048, 256)
        for k in (2, 1, 3, 0):
            part = dot(hot[k], table)
            if k == 0:
                emb[:, 256 * j : 256 * (j + 1)] = part
            else:
                psend[k, :, 256 * j : 256 * (j + 1)] = part.astype(BF16)
                part_copies[j, k] = remote(
                    "y", psend.at[k, :, chunk(j)], prec.at[4 - k, :, chunk(j)], ypeer(4 - k)
                )

    load_chroma.wait()
    chroma_hot = jnp.where(
        colt[0, :, 8:9] == iota((1, 256), 1).astype(F32), 1.0, 0.0
    ).astype(BF16)
    tok_copies = {}
    for j in (0, 1):
        cols = slice(256 * j, 256 * (j + 1))
        total = emb[:, cols] + dot(chroma_hot, chroma[:, cols])
        for k in (1, 3, 2):
            part_copies[j, k].wait_recv()
        for k in (1, 2, 3):
            total = total + prec[k, :, cols].astype(F32)
        toks[0, :, cols] = total.astype(BF16)
        for k in range(1, 8):
            tok_copies[j, k] = remote("t", toks.at[0, :, chunk(j)], toks.at[k, :, chunk(j)], tpeer(k))

    load_w.wait()
    ssq = jnp.zeros((FR, 1), F32)
    for n, k in enumerate((0, 1, 7, 2, 6, 3, 5, 4)):
        if k:
            tok_copies[0, k].wait_recv()
            tok_copies[1, k].wait_recv()
        feature = lax.rem(t + 8 - k, 8)
        block = toks[k].astype(F32)
        ssq = ssq + jnp.sum(block * block, axis=1, keepdims=True)
        gain = gains_ref[:, pl.ds(pl.multiple_of(512 * feature, 512), 512)]
        scaled = (block * gain).astype(BF16)
        for i in range(3):
            product = dot(scaled, wv[i, pl.ds(pl.multiple_of(512 * feature, 512), 512), :])
            if n == 0:
                acc[i] = product
            else:
                acc[i] += product
    dq_copies[1] = [send_dq(1, k) for k in range(1, 8)]
    dq_copies[2] = [send_dq(2, k) for k in range(1, 8)]
    dp_copies = [
        remote(
            "t",
            dproj_ref.at[pl.ds(pl.multiple_of(64 * c, 64), 64)],
            dp.at[t, c],
            tpeer(k),
        )
        for k in range(1, 8)
    ]

    factor = lax.rsqrt(ssq * (1.0 / 4096) + 1e-05)
    base_cos = bases_ref[0, pl.ds(s, 1), :]
    base_sin = bases_ref[1, pl.ds(s, 1), :]
    cosines = rows_ref[0] * base_cos - rows_ref[1] * base_sin
    sines = rows_ref[1] * base_cos + rows_ref[0] * base_sin
    sines = jnp.where(iota((1, HEAD), 1) < 64, -sines, sines)
    songs = pack_ref[9:10, :].astype(F32)
    song_row = iota((16, HEAD), 0)
    song_rows = jnp.where(
        song_row == 0, songs[:, :128], jnp.where(song_row == 1, songs[:, 128:], 0.0)
    ).astype(BF16)
    for h in range(4):
        cols = slice(HEAD * h, HEAD * (h + 1))
        for i in range(3):
            entries = acc[i, :, cols] * factor
            if i < 2:
                entries = entries * cosines + pltpu.roll(entries, 64, 1) * sines
            if i == 0:
                qs[h] = entries.astype(BF16)
            else:
                kvs[h, FR * (i - 1) : FR * i, :] = entries.astype(BF16)
        kvs[h, 2 * FR :, :] = song_rows

    load_wout = [
        local(wout_ref.at[:, pl.ds(512 * j, 512)], wv.at[0, pl.ds(512 * j, 512)]) for j in range(8)
    ]
    kv_copies = {}
    q_copies = {}
    for k in (1, 3, 2):
        head = lax.rem(y + k, 4)
        kv_copies[k] = remote("y", kvs.at[head], kvb.at[0, k], ypeer(k))
    for k in (1, 3, 2):
        head = lax.rem(y + k, 4)
        q_copies[k] = remote("y", qs.at[head], qb.at[k], ypeer(k))
    kvb[0, 0] = kvs[y]
    qb[0] = qs[y]
    kv_x = {}
    kv_s = {}
    for k in (0, 1, 3, 2):
        if k:
            kv_copies[k].wait_recv()
        kv_x[k] = remote("r", kvb.at[0, k], kvb.at[2, k], xpeer)
        kv_s[k] = remote("r", kvb.at[0, k], kvb.at[1, k], sib)
    kv_f = {}
    for k in (0, 1, 3, 2):
        kv_x[k].wait_recv()
        kv_f[k] = remote("r", kvb.at[2, k], kvb.at[3, k], sib)
    for k in (0, 1, 3, 2):
        kv_s[k].wait_recv()
        kv_f[k].wait_recv()
        if k:
            q_copies[k].wait_recv()

    scale = HEAD**-0.5
    row_id = iota((FR, 1), 0)
    col_id = iota((1, FR), 1)
    o_copies = {}
    for kq in (2, 1, 3, 0):
        yq = lax.rem(y + 4 - kq, 4)
        groups = jnp.minimum(yq + 1, 3)
        queries = qb[kq]
        query_song = colt[kq, :, 9:10]
        query_pos = FR * (4 * yq + q4) + row_id

        def scores_of(j, peak):
            yk = yq - j // 4
            r = j % 4
            kk = lax.rem(y + 4 - yk, 4)
            shard = 4 * yk + ring(r)
            tail = kvb[r, kk, 2 * FR :, :].astype(F32)
            key_song = jnp.concatenate([tail[0:1, :], tail[1:2, :]], axis=1)
            found = lax.dot_general(
                queries,
                kvb[r, kk, :FR, :],
                (((1,), (1,)), ((), ())),
                preferred_element_type=F32,
            )
            allowed = (query_song == key_song) & (query_pos >= FR * shard + col_id)
            found = jnp.where(allowed, found, -1e30)
            sbuf[j] = found
            return jnp.maximum(peak, jnp.max(found, axis=1, keepdims=True))

        peak = lax.fori_loop(0, 4 * groups, scores_of, jnp.full((FR, 1), -1e30, F32))

        def blend(j, carry):
            totals, blended = carry
            yk = yq - j // 4
            r = j % 4
            kk = lax.rem(y + 4 - yk, 4)
            weights = jnp.exp((sbuf[j] - peak) * scale)
            totals = totals + jnp.sum(weights, axis=1, keepdims=True)
            blended = blended + dot(weights.astype(BF16), kvb[r, kk, FR : 2 * FR, :])
            return totals, blended

        totals, blended = lax.fori_loop(
            0, 4 * groups, blend, (jnp.zeros((FR, 1), F32), jnp.zeros((FR, HEAD), F32))
        )
        head_cols = pl.ds(pl.multiple_of(HEAD * y, HEAD), HEAD)
        result = (blended / totals).astype(BF16)
        if kq:
            ob[kq] = result
            o_copies[kq] = remote("y", ob.at[kq], att.at[:, head_cols], ypeer(4 - kq))
        else:
            att[:, head_cols] = result
    for k in (1, 2, 3):
        o_copies[k].wait_recv()

    for copy in load_wout:
        copy.wait()
    attended = att[...]
    r_copies = {}
    for k in (4, 3, 5, 2, 6, 1, 7):
        columns = wv[0, pl.ds(pl.multiple_of(512 * blk(k), 512), 512), :]
        rsend[k] = dot(attended, columns).astype(BF16)
        r_copies[k] = remote("t", rsend.at[k], rrec.at[k], tpeer(k))
    total = toks[0].astype(F32) + dot(
        attended, wv[0, pl.ds(pl.multiple_of(512 * t, 512), 512), :]
    )
    emb[...] = total

    load_di.wait()
    load_dq.wait()
    load_dp.wait()
    for copy in di_copies:
        copy.wait_recv()
    di_forward = remote("r", di.at[di_half], di.at[di_half], sib)
    dq_forward = []
    for i in range(3):
        for copy in dq_copies[i]:
            copy.wait_recv()
        dq_forward.append(remote("r", dq.at[i, half], dq.at[i, half], sib))
    for copy in dp_copies:
        copy.wait_recv()
    dp_forward = remote("r", dp.at[:, c], dp.at[:, c], sib)

    for k in (1, 7, 2, 6, 3, 5, 4):
        r_copies[k].wait_recv()
        emb[...] += rrec[k].astype(F32)
    thl[...] = emb[...].astype(BF16)
    th_copies = [
        remote(
            "t",
            thl.at[pl.ds(pl.multiple_of(OWN * blk(k), OWN), OWN)],
            thb.at[:, pl.ds(pl.multiple_of(512 * t, 512), 512)],
            tpeer(k),
        )
        for k in range(1, 8)
    ]
    hidden = thl[...].astype(F32)
    square = jnp.sum(hidden * hidden, axis=1, keepdims=True)
    high = square.astype(BF16).astype(F32)
    middle = (square - high).astype(BF16).astype(F32)
    low = square - high - middle
    place = iota((FR, HEAD), 1)
    squares = jnp.where(
        place == 0, high, jnp.where(place == 1, middle, jnp.where(place == 2, low, 0.0))
    )
    pfull[:, :, 1024:] = squares.astype(BF16).reshape(8, OWN, HEAD)
    gain = gains_ref[:, pl.ds(pl.multiple_of(4096 + 512 * t, 512), 512)]
    scaled = (hidden * gain).astype(BF16)
    di_forward.wait_recv()
    for j in range(2):
        cols = slice(512 * j, 512 * (j + 1))
        pfull[:, :, cols] = dot(scaled, di[:, cols]).astype(BF16).reshape(8, OWN, 512)
    p_copies = [remote("t", pfull.at[blk(k)], prb.at[k], tpeer(k)) for k in range(1, 8)]
    thb[:, pl.ds(pl.multiple_of(512 * t, 512), 512)] = thl[
        pl.ds(pl.multiple_of(OWN * t, OWN), OWN), :
    ]

    summed = pfull[t].astype(F32)
    for copy in lk_copies:
        copy.wait_recv()
    for k in range(1, 8):
        p_copies[k - 1].wait_recv()
        summed = summed + prb[k].astype(F32)
    square = jnp.sum(summed[:, 1024:], axis=1, keepdims=True)
    projected = summed[:, :1024] * lax.rsqrt(square * (1.0 / 4096) + 1e-05)
    inputs = [projected.astype(BF16)]
    for b in range(7):
        inputs.append((projected + lkf[b].astype(F32)).astype(BF16))
    by_book = jnp.concatenate(inputs, axis=0)
    out_row = iota((FR, FR), 0)
    order = jnp.where(
        iota((FR, FR), 1) == (out_row % 8) * OWN + out_row // 8, 1.0, 0.0
    ).astype(BF16)
    inputs = dot(order, by_book)
    factor = lax.rsqrt(jnp.mean(inputs * inputs, axis=1, keepdims=True) + 1e-05)
    normed = (inputs * factor * gains_ref[:, 8192:]).astype(BF16)
    for copy in dq_forward:
        copy.wait_recv()
    depth_q, depth_k, depth_v = [dot(normed, dq[i]).astype(BF16) for i in range(3)]
    left = iota((1, 128), 1) < DHEAD
    seen_row = iota((256, 128), 0) % 128
    seen_col = iota((256, 128), 1)
    seen = (seen_col <= seen_row) & (seen_col >= (seen_row // 8) * 8)
    zero = jnp.zeros((), BF16)
    for p in range(8):
        cols = slice(128 * p, 128 * (p + 1))
        for g in range(2):
            rows = slice(128 * g, 128 * (g + 1))
            pair = depth_q[rows, cols]
            both = jnp.concatenate([jnp.where(left, pair, zero), jnp.where(left, zero, pair)], axis=0)
            found = lax.dot_general(
                both,
                depth_k[rows, cols],
                (((1,), (1,)), ((), ())),
                preferred_element_type=F32,
            )
            found = jnp.where(seen, found, -1e30)
            peak = jnp.max(found, axis=1, keepdims=True)
            weights = jnp.exp((found - peak) * DHEAD**-0.5)
            totals = jnp.sum(weights, axis=1, keepdims=True)
            blended = dot(weights.astype(BF16), depth_v[rows, cols]) / totals
            mixed[rows, cols] = jnp.where(left, blended[:128], blended[128:]).astype(BF16)
    dp_forward.wait_recv()
    dh_out[...] = (inputs + dot(mixed[...], dp[...].reshape(1024, 1024))).astype(BF16)

    for copy in th_copies:
        copy.wait_recv()
    th_out[...] = thb[...]
    for copy in pending:
        copy.wait_send()


def shards(
    audio_codes,
    chroma_ids,
    song_ids,
    code_table,
    chroma_table,
    attention_gain,
    temporal_qkv,
    temporal_out,
    output_gain,
    depth_input,
    depth_table,
    depth_gain,
    depth_qkv,
    depth_proj,
):
    pack = jnp.concatenate(
        [
            audio_codes.T,
            chroma_ids[None],
            song_ids[None],
            jnp.zeros((6, FR), jnp.int32),
        ],
        axis=0,
    )
    gains = jnp.concatenate([attention_gain, output_gain, depth_gain])[None]
    rows, bases = rotation_tables()
    vmem = pl.BlockSpec(memory_space=pltpu.VMEM)
    anywhere = pl.BlockSpec(memory_space=pl.ANY)
    temporal, depth = pl.pallas_call(
        kernel,
        out_shape=(
            jax.ShapeDtypeStruct((OWN, 4096), BF16),
            jax.ShapeDtypeStruct((FR, 1024), BF16),
        ),
        in_specs=[vmem] * 4 + [anywhere] * 8,
        out_specs=(vmem, vmem),
        scratch_shapes=[
            pltpu.VMEM((3, 4096, 512), BF16),
            pltpu.VMEM((8, 4, 64, 512), BF16),
            pltpu.VMEM((4, FR, 2048), BF16),
            pltpu.VMEM((256, 512), BF16),
            pltpu.VMEM((7, 1024, 128), BF16),
            pltpu.VMEM((7, FR, 128), BF16),
            pltpu.VMEM((7, OWN, 1024), BF16),
            pltpu.VMEM((4, 16, FR), jnp.int32),
            pltpu.VMEM((4, FR, 16), F32),
            pltpu.VMEM((FR, 512), F32),
            pltpu.VMEM((4, FR, 512), BF16),
            pltpu.VMEM((4, FR, 512), BF16),
            pltpu.VMEM((8, FR, 512), BF16),
            pltpu.VMEM((3, FR, 512), F32),
            pltpu.VMEM((4, PIECE, HEAD), BF16),
            pltpu.VMEM((4, 4, PIECE, HEAD), BF16),
            pltpu.VMEM((4, FR, HEAD), BF16),
            pltpu.VMEM((4, FR, HEAD), BF16),
            pltpu.VMEM((12, FR, FR), F32),
            pltpu.VMEM((4, FR, HEAD), BF16),
            pltpu.VMEM((FR, 512), BF16),
            pltpu.VMEM((8, FR, 512), BF16),
            pltpu.VMEM((8, FR, 512), BF16),
            pltpu.VMEM((FR, 512), BF16),
            pltpu.VMEM((OWN, 4096), BF16),
            pltpu.VMEM((512, 1024), BF16),
            pltpu.VMEM((8, OWN, 1152), BF16),
            pltpu.VMEM((8, OWN, 1152), BF16),
            pltpu.VMEM((3, 1024, 1024), BF16),
            pltpu.VMEM((8, 2, 64, 1024), BF16),
            pltpu.VMEM((FR, 1024), BF16),
            pltpu.SemaphoreType.DMA((15,)),
            pltpu.SemaphoreType.DMA((18,)),
            pltpu.SemaphoreType.DMA((18,)),
            pltpu.SemaphoreType.DMA((23,)),
            pltpu.SemaphoreType.DMA((23,)),
            pltpu.SemaphoreType.DMA((77,)),
            pltpu.SemaphoreType.DMA((77,)),
        ],
        compiler_params=pltpu.CompilerParams(
            collective_id=0, has_side_effects=True, vmem_limit_bytes=60 * 1024 * 1024
        ),
        name="layer",
    )(
        pack,
        gains,
        rows,
        bases,
        code_table,
        chroma_table,
        temporal_qkv,
        temporal_out,
        depth_input,
        depth_table,
        depth_qkv,
        depth_proj,
    )
    return temporal, depth.reshape(OWN, 8, 1024)


def solution(mesh):
    placed = (
        P("seq", None),
        P("seq"),
        P("seq"),
        P(None, "seq", "tensor"),
        P(None, "tensor"),
        P(),
        P(None, None, "tensor"),
        P("tensor", None),
        P(),
        P(None, "tensor"),
        P(None, None, "tensor"),
        P(),
        P(None, None, "tensor"),
        P("tensor", None),
    )
    return jax.shard_map(
        shards,
        mesh=mesh,
        in_specs=placed,
        out_specs=(P(("seq", "tensor"), None), P(("seq", "tensor"), None, None)),
        check_vma=False,
    )
```

time: 687 us -> 189 us (0.28)
  waiting for transfers between devices: 522 us -> 0 us
  Pallas kernels: 0 us -> 182 us
  local copies, waits for them, and re-layouts: 64.1 us -> 3.61 us
  matrix products: 50.3 us -> 0 us
  blocking collectives: 19.6 us -> 0 us
  between operations: 15.1 us -> 0.65 us
  other arithmetic: 13.9 us -> 2.77 us
    all_gather x8 -> x0, waiting for transfers between devices: 448 us -> none  [the longest x1 114 us: shards(): lax.all_gather(depth_input, 'tensor', axis=1, tiled=True)]
    pallas_call x0 -> x1, Pallas kernels: none -> 182 us  [shards(): pl.pallas_call(kernel, out_shape=(jax.ShapeDtypeStruct((OWN, 4096), BF16)...]
    reduce_scatter x1 -> x0, waiting for transfers between devices: 71.9 us -> none  [shards(): lax.psum_scatter(jnp.dot(attended, temporal_out, preferred_element_type=j...]
    dot_general x14 -> x0, matrix products: 50.3 us -> none  [the longest x1 7.5 us: update(): jnp.einsum('qhk,khd->qhd', weights.astype(jnp.bfloat16), block_values.res...]
    gather x15 -> x0, local copies, waits for them, and re-layouts: 27.2 us -> none  [the longest x8 21.2 us: look_up(): jnp.take(tables[codebook], offsets[:, codebook], axis=0).astype(jnp.float32)]
    dot_general x4 -> x0, local copies, waits for them, and re-layouts: 19.9 us -> none  [the longest x2 12.3 us: shards(): jnp.dot(normed, temporal_qkv[0], preferred_element_type=jnp.float32)]
    all_gather x1 -> x0, blocking collectives: 19.6 us -> none  [shards(): block_songs = lax.all_gather(song_ids, 'seq', axis=0, tiled=True)]
    squeeze x2 -> x0, local copies, waits for them, and re-layouts: 7.21 us -> none  [the longest x1 5.66 us: look_up(): tables[codebook]]
  transfers between devices with their start and end apart: 9 -> 0, of which waited for: 9 -> 0; matrix products, arithmetic and copies ran while one was open for 9% -> 0% of each run, Pallas kernels for 0% -> 0%
where the time goes in v1:
time: 189 us
  Pallas kernels  182 us (96%)
  local copies, waits for them, and re-layouts  3.61 us (2%)
  other arithmetic  2.77 us (1%)
    pallas_call x1, Pallas kernels, shards(): pl.pallas_call(kernel, out_shape=(jax.ShapeDtypeStruct((OWN, 4096), BF16)...  182 us

profile of v1, /device:TPU:1, one launch (start us, length us, event | category | flops | bytes accessed | tf_op | source)
XLA Modules:
  0.0 188.9 jit_solution(16518623155744073084)
XLA Ops:
  0.6 0.1 pad.6.clone
  0.7 1.4 add_add_fusion.pack_ref
  2.1 1.4 pad_maximum_fusion
  3.5 181.8 %layer.1 = (bf16[32,4096]{1,0:T(8,128)(2,1)}, bf16[256,1024]{1,0:T(8,128)(2,1)}) custom-call(s32[16,256]{1,0:T(8,128)} %add_add_fusion.pack_ref, f32[1,9216]{1,0:T(1,128)} %bitcast.6, f32[2,256,128]{2,1,0:T(8,128)} %constant.6.clone.rows_ref, f32[2,16,128]{2,1,0:T(8,128)} %constant.7.clone.bases_ref, bf16[8,64,512]{2,1,0:T(8,128)(2,1)} %ctab_ref.1, ...), custom_call_target="tpu_custom_call" | custom-call | tf_op jit(solution)/shard_map/layer/pallas_call | solution.py:540
  185.3 1.7 copy.20
  187.0 1.9 copy.21
  (1 shorter events, 0.0 us)

commit v2 on v1

--- a/solution.py
+++ b/solution.py
@@ -37,8 +37,12 @@
 
 
 def kernel(
-    pack_ref,
-    gains_ref,
+    codes_ref,
+    chroma_ids_ref,
+    songs_ref,
+    again_ref,
+    ogain_ref,
+    dgain_ref,
     rows_ref,
     bases_ref,
     ctab_ref,
@@ -146,17 +150,22 @@
     load_tab = local(ctab_ref, tab.at[:, 0])
     load_chroma = local(chroma_ref, chroma)
     load_w = local(wqkv_ref, wv)
-    half = pl.ds(pl.multiple_of(512 * c, 512), 512)
     own_cols = pl.ds(pl.multiple_of(128 * t, 128), 128)
-    load_dq = local(dqkv_ref.at[:, half], dq.at[:, half, own_cols])
-    load_dp = local(
-        dproj_ref.at[pl.ds(pl.multiple_of(64 * c, 64), 64)],
-        dp.at[t, c],
-    )
+    dq_half = pl.ds(pl.multiple_of(512 * c, 512), 512)
+    dq_part = pl.ds(pl.multiple_of(512 * c + 128 * y, 128), 128)
+    dp_part = pl.ds(pl.multiple_of(64 * c + 16 * y, 16), 16)
     di_half = pl.ds(pl.multiple_of(256 * c, 256), 256)
-    load_di = local(
-        din_ref.at[pl.ds(pl.multiple_of(512 * t + 256 * c, 256), 256)],
-        di.at[di_half, own_cols],
+    di_part = pl.ds(pl.multiple_of(256 * c + 64 * y, 64), 64)
+
+    def di_of(block):
+        return din_ref.at[pl.ds(pl.multiple_of(512 * block + 256 * c + 64 * y, 64), 64)]
+
+    load_dq = local(dqkv_ref.at[:, dq_part], dq.at[:, dq_part, own_cols])
+    load_dp = local(dproj_ref.at[dp_part], dp.at[t, c, y])
+    load_di = local(di_of(t), di.at[di_part, own_cols])
+
+    cpb[0] = jnp.concatenate(
+        [codes_ref[...], chroma_ids_ref[...], songs_ref[...], jnp.zeros((6, FR), jnp.int32)], axis=0
     )
 
     barrier = pltpu.get_barrier_semaphore()
@@ -165,8 +174,7 @@
         pl.semaphore_signal(barrier, inc=1, device_id=device, device_id_type=MESH)
     pl.semaphore_wait(barrier, len(greeted))
 
-    cpb[0] = pack_ref[...]
-    code_copies = {k: remote("y", pack_ref, cpb.at[k], ypeer(k)) for k in (1, 2, 3)}
+    code_copies = {k: remote("y", cpb.at[0], cpb.at[k], ypeer(k)) for k in (1, 2, 3)}
     chunk = lambda j: pl.ds(256 * j, 256)
     tab_x = [
         remote("r", ctab_ref.at[:, :, chunk(j)], tab.at[:, 2, :, chunk(j)], xpeer) for j in (0, 1)
@@ -175,38 +183,7 @@
         remote("r", ctab_ref.at[:, :, chunk(j)], tab.at[:, 1, :, chunk(j)], sib) for j in (0, 1)
     ]
 
-    def send_di(k):
-        return remote(
-            "t",
-            din_ref.at[pl.ds(pl.multiple_of(512 * blk(k) + 256 * c, 256), 256)],
-            di.at[di_half, own_cols],
-            tpeer(k),
-        )
-
-    def send_dq(i, k):
-        return remote("t", dqkv_ref.at[i, half], dq.at[i, half, own_cols], tpeer(k))
-
-    di_copies = [send_di(k) for k in range(1, 8)]
-    dq_copies = {0: [send_dq(0, k) for k in range(1, 8)]}
-
-    cpb_own = pack_ref[...].astype(F32)
-    own_cols_t = jnp.transpose(cpb_own)
-    colt[0] = own_cols_t
-    load_dtab.wait()
-    entry = iota((1, 1024), 1).astype(F32)
-    for b in range(7):
-        onehot = jnp.where(colt[0, :, b : b + 1] == entry, 1.0, 0.0).astype(BF16)
-        lk[b] = dot(onehot, dtab[b]).astype(BF16)
-    lk_copies = [
-        remote(
-            "t",
-            lk.at[:, pl.ds(pl.multiple_of(OWN * blk(k), OWN), OWN)],
-            lkf.at[:, :, own_cols],
-            tpeer(k),
-        )
-        for k in range(1, 8)
-    ]
-    lkf[:, :, own_cols] = lk[:, pl.ds(pl.multiple_of(OWN * t, OWN), OWN)]
+    colt[0] = jnp.transpose(cpb[0].astype(F32))
 
     lane = iota((1, 256), 1)
     lane_q = 2 * lax.rem(x + lane // 128, 2) + lax.rem(c + (lane // 64) % 2, 2)
@@ -222,7 +199,6 @@
     load_tab.wait()
 
     part_copies = {}
-    forwards = []
     for j in (0, 1):
         tab_x[j].wait_recv()
         forward = remote("r", tab.at[:, 2, :, chunk(j)], tab.at[:, 3, :, chunk(j)], sib)
@@ -239,6 +215,12 @@
                     "y", psend.at[k, :, chunk(j)], prec.at[4 - k, :, chunk(j)], ypeer(4 - k)
                 )
 
+    di_copies = [remote("t", di_of(blk(k)), di.at[di_part, own_cols], tpeer(k)) for k in range(1, 8)]
+    dqa_copies = [
+        remote("t", dqkv_ref.at[0:2, dq_part], dq.at[0:2, dq_part, own_cols], tpeer(k))
+        for k in range(1, 8)
+    ]
+
     load_chroma.wait()
     chroma_hot = jnp.where(
         colt[0, :, 8:9] == iota((1, 256), 1).astype(F32), 1.0, 0.0
@@ -255,6 +237,24 @@
         for k in range(1, 8):
             tok_copies[j, k] = remote("t", toks.at[0, :, chunk(j)], toks.at[k, :, chunk(j)], tpeer(k))
 
+    load_dtab.wait()
+    entry = iota((1, 1024), 1).astype(F32)
+    for b in range(7):
+        onehot = jnp.where(colt[0, :, b : b + 1] == entry, 1.0, 0.0).astype(BF16)
+        lk[b] = dot(onehot, dtab[b]).astype(BF16)
+    lkf[:, :, own_cols] = lk[:, pl.ds(pl.multiple_of(OWN * t, OWN), OWN)]
+
+    load_di.wait()
+    load_dq.wait()
+    for copy in di_copies:
+        copy.wait_recv()
+    di_y = [remote("y", di.at[di_part], di.at[di_part], ypeer(k)) for k in (1, 3, 2)]
+    for copy in dqa_copies:
+        copy.wait_recv()
+    dqa_y = [
+        remote("y", dq.at[0:2, dq_part], dq.at[0:2, dq_part], ypeer(k)) for k in (1, 3, 2)
+    ]
+
     load_w.wait()
     ssq = jnp.zeros((FR, 1), F32)
     for n, k in enumerate((0, 1, 7, 2, 6, 3, 5, 4)):
@@ -264,7 +264,7 @@
         feature = lax.rem(t + 8 - k, 8)
         block = toks[k].astype(F32)
         ssq = ssq + jnp.sum(block * block, axis=1, keepdims=True)
-        gain = gains_ref[:, pl.ds(pl.multiple_of(512 * feature, 512), 512)]
+        gain = again_ref[:, pl.ds(pl.multiple_of(512 * feature, 512), 512)]
         scaled = (block * gain).astype(BF16)
         for i in range(3):
             product = dot(scaled, wv[i, pl.ds(pl.multiple_of(512 * feature, 512), 512), :])
@@ -272,25 +272,13 @@
                 acc[i] = product
             else:
                 acc[i] += product
-    dq_copies[1] = [send_dq(1, k) for k in range(1, 8)]
-    dq_copies[2] = [send_dq(2, k) for k in range(1, 8)]
-    dp_copies = [
-        remote(
-            "t",
-            dproj_ref.at[pl.ds(pl.multiple_of(64 * c, 64), 64)],
-            dp.at[t, c],
-            tpeer(k),
-        )
-        for k in range(1, 8)
-    ]
-
     factor = lax.rsqrt(ssq * (1.0 / 4096) + 1e-05)
     base_cos = bases_ref[0, pl.ds(s, 1), :]
     base_sin = bases_ref[1, pl.ds(s, 1), :]
     cosines = rows_ref[0] * base_cos - rows_ref[1] * base_sin
     sines = rows_ref[1] * base_cos + rows_ref[0] * base_sin
     sines = jnp.where(iota((1, HEAD), 1) < 64, -sines, sines)
-    songs = pack_ref[9:10, :].astype(F32)
+    songs = songs_ref[...].astype(F32)
     song_row = iota((16, HEAD), 0)
     song_rows = jnp.where(
         song_row == 0, songs[:, :128], jnp.where(song_row == 1, songs[:, 128:], 0.0)
@@ -337,50 +325,72 @@
         if k:
             q_copies[k].wait_recv()
 
-    scale = HEAD**-0.5
-    row_id = iota((FR, 1), 0)
-    col_id = iota((1, FR), 1)
+    lk_copies = [
+        remote(
+            "t",
+            lk.at[:, pl.ds(pl.multiple_of(OWN * blk(k), OWN), OWN)],
+            lkf.at[:, :, own_cols],
+            tpeer(k),
+        )
+        for k in range(1, 8)
+    ]
+    dqb_copies = [
+        remote("t", dqkv_ref.at[2, dq_part], dq.at[2, dq_part, own_cols], tpeer(k))
+        for k in range(1, 8)
+    ]
+    dp_copies = [remote("t", dproj_ref.at[dp_part], dp.at[t, c, y], tpeer(k)) for k in range(1, 8)]
+
+    scale = HEAD**-0.5 * float(np.log2(np.e))
+    behind = iota((FR, FR), 1) - iota((FR, FR), 0)
     o_copies = {}
     for kq in (2, 1, 3, 0):
         yq = lax.rem(y + 4 - kq, 4)
-        groups = jnp.minimum(yq + 1, 3)
+        earlier = jnp.minimum(yq, 2)
         queries = qb[kq]
-        query_song = colt[kq, :, 9:10]
-        query_pos = FR * (4 * yq + q4) + row_id
-
-        def scores_of(j, peak):
-            yk = yq - j // 4
-            r = j % 4
-            kk = lax.rem(y + 4 - yk, 4)
-            shard = 4 * yk + ring(r)
+        query_song = jnp.broadcast_to(colt[kq, :, 9:10], (FR, HEAD))
+
+        def scores_of(group, r, kk, same_row):
             tail = kvb[r, kk, 2 * FR :, :].astype(F32)
-            key_song = jnp.concatenate([tail[0:1, :], tail[1:2, :]], axis=1)
             found = lax.dot_general(
                 queries,
                 kvb[r, kk, :FR, :],
                 (((1,), (1,)), ((), ())),
                 preferred_element_type=F32,
             )
-            allowed = (query_song == key_song) & (query_pos >= FR * shard + col_id)
+            allowed = jnp.concatenate(
+                [query_song == tail[0:1, :], query_song == tail[1:2, :]], axis=1
+            )
+            if same_row:
+                allowed = allowed & (behind <= FR * (q4 - ring(r)))
             found = jnp.where(allowed, found, -1e30)
-            sbuf[j] = found
-            return jnp.maximum(peak, jnp.max(found, axis=1, keepdims=True))
-
-        peak = lax.fori_loop(0, 4 * groups, scores_of, jnp.full((FR, 1), -1e30, F32))
-
-        def blend(j, carry):
+            sbuf[4 * group + r] = found
+            return jnp.maximum(found[:, :HEAD], found[:, HEAD:])
+
+        def highest_of(group, highest, same_row):
+            kk = lax.rem(kq + group, 4)
+            for r in range(4):
+                highest = jnp.maximum(highest, scores_of(group, r, kk, same_row))
+            return highest
+
+        highest = highest_of(0, jnp.full((FR, HEAD), -1e30, F32), True)
+        highest = lax.fori_loop(
+            1, earlier + 1, lambda group, carry: highest_of(group, carry, False), highest
+        )
+        peak = jnp.max(highest, axis=1, keepdims=True) * scale
+
+        def blend(group, carry):
             totals, blended = carry
-            yk = yq - j // 4
-            r = j % 4
-            kk = lax.rem(y + 4 - yk, 4)
-            weights = jnp.exp((sbuf[j] - peak) * scale)
-            totals = totals + jnp.sum(weights, axis=1, keepdims=True)
-            blended = blended + dot(weights.astype(BF16), kvb[r, kk, FR : 2 * FR, :])
+            kk = lax.rem(kq + group, 4)
+            for r in range(4):
+                weights = jnp.exp2(sbuf[4 * group + r] * scale - peak)
+                totals = totals + (weights[:, :HEAD] + weights[:, HEAD:])
+                blended = blended + dot(weights.astype(BF16), kvb[r, kk, FR : 2 * FR, :])
             return totals, blended
 
         totals, blended = lax.fori_loop(
-            0, 4 * groups, blend, (jnp.zeros((FR, 1), F32), jnp.zeros((FR, HEAD), F32))
+            0, earlier + 1, blend, (jnp.zeros((FR, HEAD), F32), jnp.zeros((FR, HEAD), F32))
         )
+        totals = jnp.sum(totals, axis=1, keepdims=True)
         head_cols = pl.ds(pl.multiple_of(HEAD * y, HEAD), HEAD)
         result = (blended / totals).astype(BF16)
         if kq:
@@ -404,34 +414,22 @@
     )
     emb[...] = total
 
-    load_di.wait()
-    load_dq.wait()
     load_dp.wait()
-    for copy in di_copies:
+    for copy in dqb_copies + dp_copies:
+        copy.wait_recv()
+    dqb_y = [remote("y", dq.at[2, dq_part], dq.at[2, dq_part], ypeer(k)) for k in (1, 3, 2)]
+    dp_y = [remote("y", dp.at[:, c, y], dp.at[:, c, y], ypeer(k)) for k in (1, 3, 2)]
+    for copy in di_y:
         copy.wait_recv()
     di_forward = remote("r", di.at[di_half], di.at[di_half], sib)
-    dq_forward = []
-    for i in range(3):
-        for copy in dq_copies[i]:
-            copy.wait_recv()
-        dq_forward.append(remote("r", dq.at[i, half], dq.at[i, half], sib))
-    for copy in dp_copies:
-        copy.wait_recv()
-    dp_forward = remote("r", dp.at[:, c], dp.at[:, c], sib)
+    for copy in dqa_y:
+        copy.wait_recv()
+    dqa_forward = remote("r", dq.at[0:2, dq_half], dq.at[0:2, dq_half], sib)
 
     for k in (1, 7, 2, 6, 3, 5, 4):
         r_copies[k].wait_recv()
         emb[...] += rrec[k].astype(F32)
     thl[...] = emb[...].astype(BF16)
-    th_copies = [
-        remote(
-            "t",
-            thl.at[pl.ds(pl.multiple_of(OWN * blk(k), OWN), OWN)],
-            thb.at[:, pl.ds(pl.multiple_of(512 * t, 512), 512)],
-            tpeer(k),
-        )
-        for k in range(1, 8)
-    ]
     hidden = thl[...].astype(F32)
     square = jnp.sum(hidden * hidden, axis=1, keepdims=True)
     high = square.astype(BF16).astype(F32)
@@ -442,16 +440,32 @@
         place == 0, high, jnp.where(place == 1, middle, jnp.where(place == 2, low, 0.0))
     )
     pfull[:, :, 1024:] = squares.astype(BF16).reshape(8, OWN, HEAD)
-    gain = gains_ref[:, pl.ds(pl.multiple_of(4096 + 512 * t, 512), 512)]
+    gain = ogain_ref[:, pl.ds(pl.multiple_of(512 * t, 512), 512)]
     scaled = (hidden * gain).astype(BF16)
     di_forward.wait_recv()
     for j in range(2):
         cols = slice(512 * j, 512 * (j + 1))
         pfull[:, :, cols] = dot(scaled, di[:, cols]).astype(BF16).reshape(8, OWN, 512)
     p_copies = [remote("t", pfull.at[blk(k)], prb.at[k], tpeer(k)) for k in range(1, 8)]
+    th_copies = [
+        remote(
+            "t",
+            thl.at[pl.ds(pl.multiple_of(OWN * blk(k), OWN), OWN)],
+            thb.at[:, pl.ds(pl.multiple_of(512 * t, 512), 512)],
+            tpeer(k),
+        )
+        for k in range(1, 8)
+    ]
     thb[:, pl.ds(pl.multiple_of(512 * t, 512), 512)] = thl[
         pl.ds(pl.multiple_of(OWN * t, OWN), OWN), :
     ]
+
+    for copy in dqb_y:
+        copy.wait_recv()
+    dqb_forward = remote("r", dq.at[2, dq_half], dq.at[2, dq_half], sib)
+    for copy in dp_y:
+        copy.wait_recv()
+    dp_forward = remote("r", dp.at[:, c], dp.at[:, c], sib)
 
     summed = pfull[t].astype(F32)
     for copy in lk_copies:
@@ -471,9 +485,9 @@
     ).astype(BF16)
     inputs = dot(order, by_book)
     factor = lax.rsqrt(jnp.mean(inputs * inputs, axis=1, keepdims=True) + 1e-05)
-    normed = (inputs * factor * gains_ref[:, 8192:]).astype(BF16)
-    for copy in dq_forward:
-        copy.wait_recv()
+    normed = (inputs * factor * dgain_ref[...]).astype(BF16)
+    dqa_forward.wait_recv()
+    dqb_forward.wait_recv()
     depth_q, depth_k, depth_v = [dot(normed, dq[i]).astype(BF16) for i in range(3)]
     left = iota((1, 128), 1) < DHEAD
     seen_row = iota((256, 128), 0) % 128
@@ -524,16 +538,6 @@
     depth_qkv,
     depth_proj,
 ):
-    pack = jnp.concatenate(
-        [
-            audio_codes.T,
-            chroma_ids[None],
-            song_ids[None],
-            jnp.zeros((6, FR), jnp.int32),
-        ],
-        axis=0,
-    )
-    gains = jnp.concatenate([attention_gain, output_gain, depth_gain])[None]
     rows, bases = rotation_tables()
     vmem = pl.BlockSpec(memory_space=pltpu.VMEM)
     anywhere = pl.BlockSpec(memory_space=pl.ANY)
@@ -543,7 +547,7 @@
             jax.ShapeDtypeStruct((OWN, 4096), BF16),
             jax.ShapeDtypeStruct((FR, 1024), BF16),
         ),
-        in_specs=[vmem] * 4 + [anywhere] * 8,
+        in_specs=[vmem] * 8 + [anywhere] * 8,
         out_specs=(vmem, vmem),
         scratch_shapes=[
             pltpu.VMEM((3, 4096, 512), BF16),
@@ -575,13 +579,13 @@
             pltpu.VMEM((8, OWN, 1152), BF16),
             pltpu.VMEM((8, OWN, 1152), BF16),
             pltpu.VMEM((3, 1024, 1024), BF16),
-            pltpu.VMEM((8, 2, 64, 1024), BF16),
+            pltpu.VMEM((8, 2, 4, 16, 1024), BF16),
             pltpu.VMEM((FR, 1024), BF16),
             pltpu.SemaphoreType.DMA((15,)),
-            pltpu.SemaphoreType.DMA((18,)),
-            pltpu.SemaphoreType.DMA((18,)),
-            pltpu.SemaphoreType.DMA((23,)),
-            pltpu.SemaphoreType.DMA((23,)),
+            pltpu.SemaphoreType.DMA((30,)),
+            pltpu.SemaphoreType.DMA((30,)),
+            pltpu.SemaphoreType.DMA((22,)),
+            pltpu.SemaphoreType.DMA((22,)),
             pltpu.SemaphoreType.DMA((77,)),
             pltpu.SemaphoreType.DMA((77,)),
         ],
@@ -590,8 +594,12 @@
         ),
         name="layer",
     )(
-        pack,
-        gains,
+        audio_codes.T,
+        chroma_ids[None],
+        song_ids[None],
+        attention_gain[None],
+        output_gain[None],
+        depth_gain[None],
         rows,
         bases,
         code_table,

time: 189 us -> 139 us (0.74)
  Pallas kernels: 182 us -> 134 us
  other arithmetic: 2.77 us -> 0 us
    pallas_call x1, Pallas kernels: 182 us -> 134 us  [shards(): pl.pallas_call(kernel, out_shape=(jax.ShapeDtypeStruct((OWN, 4096), BF16)...]
    concatenate x2 -> x0, other arithmetic: 2.77 us -> none  [the longest x1 1.41 us: shards(): jnp.concatenate([audio_codes.T, chroma_ids[None], song_ids[None], jnp.zer...]
where the time goes in v2:
time: 139 us
  Pallas kernels  134 us (96%)
  local copies, waits for them, and re-layouts  3.54 us (3%)
    pallas_call x1, Pallas kernels, shards(): pl.pallas_call(kernel, out_shape=(jax.ShapeDtypeStruct((OWN, 4096), BF16)...  134 us
    unnamed x2, local copies, waits for them, and re-layouts  3.54 us

profile of v2, /device:TPU:1, one launch (start us, length us, event | category | flops | bytes accessed | tf_op | source)
XLA Modules:
  0.0 138.6 jit_solution(5897792621552761083)
XLA Ops:
  0.6 134.4 %layer.1 = (bf16[32,4096]{1,0:T(8,128)(2,1)}, bf16[256,1024]{1,0:T(8,128)(2,1)}) custom-call(s32[8,256]{1,0:T(8,128)} %bitcast.10, s32[1,256]{1,0:T(1,128)} %bitcast.12, s32[1,256]{1,0:T(1,128)} %bitcast.13, f32[1,4096]{1,0:T(1,128)} %bitcast.8, f32[1,4096]{1,0:T(1,128)} %bitcast.9, f32[1,1024]{1,0:T(1,128)} %bitcast.11, ...), custom_call_target="tpu_custom_call" | custom-call | tf_op jit(solution)/shard_map/layer/pallas_call | solution.py:544
  135.0 1.7 %copy.20 = bf16[32,4096]{1,0:T(8,128)(2,1)} copy(bf16[32,4096]{1,0:T(8,128)(2,1)} %get-tuple-element.8) | data formatting | bytes 524288
  136.7 1.9 %copy.21 = bf16[32,8,1024]{2,1,0:T(8,128)(2,1)} copy(bf16[32,8,1024]{2,1,0:T(8,128)(2,1)} %bitcast.7) | data formatting | bytes 1048576

commit v3 on v2

v3 whole, which is shorter than its diff:
```python
import functools

import jax
import jax.numpy as jnp
import numpy as np
from jax import lax
from jax.experimental import pallas as pl
from jax.experimental.pallas import tpu as pltpu
from jax.sharding import PartitionSpec as P

MESH = pl.DeviceIdType.MESH
F32 = jnp.float32
BF16 = jnp.bfloat16
HEAD = 128
DHEAD = 64
FR = 256
OWN = 32
HR = FR // 2
HALF = OWN // 2
PIECE = 3 * HR + 16


def rotation_tables():
    freq = 10000.0 ** (-(np.arange(64, dtype=np.float64) * 2.0 / HEAD))
    frames = np.arange(FR, dtype=np.float64).reshape(8, 2, HALF).transpose(1, 0, 2).reshape(FR)
    row = frames[:, None] * freq[None]
    base = np.arange(16, dtype=np.float64)[:, None] * FR * freq[None]
    wide = lambda entries: np.concatenate([entries, entries], axis=1)
    rows = np.stack([wide(np.cos(row)), wide(np.sin(row))])
    bases = np.stack([wide(np.cos(base)), wide(np.sin(base))])
    return rows.astype(np.float32), bases.astype(np.float32)


def dot(a, b):
    return jnp.dot(a, b, preferred_element_type=F32)


def iota(shape, axis):
    return lax.broadcasted_iota(jnp.int32, shape, axis)


def kernel(
    codes_ref,
    chroma_ids_ref,
    songs_ref,
    again_ref,
    ogain_ref,
    dgain_ref,
    rows_ref,
    bases_ref,
    ctab_ref,
    chroma_ref,
    wqkv_ref,
    wout_ref,
    din_ref,
    dtab_ref,
    dqkv_ref,
    dproj_ref,
    th_out,
    dh_out,
    wv,
    tab,
    hot,
    chroma,
    dtab,
    lk,
    lkf,
    cpb,
    colt,
    emb,
    resid,
    psend,
    prec,
    toks,
    acc,
    kvs,
    kvb,
    sbuf,
    ob,
    att,
    rsend,
    rrec,
    thl,
    thb,
    di,
    pfull,
    prb,
    dq,
    dp,
    mixed,
    lsem,
    ysend,
    yrecv,
    rowsend,
    rowrecv,
    tsend,
    trecv,
):
    s = lax.axis_index("seq")
    t = lax.axis_index("tensor")
    y = s // 4
    x = (s // 2) % 2
    c = s % 2
    q4 = s % 4

    def ypeer(k):
        return (lax.rem(y + k, 4) * 4 + q4, t)

    sib = (y * 4 + x * 2 + (1 - c), t)
    xpeer = (y * 4 + (1 - x) * 2 + c, t)

    def tpeer(k):
        return (s, lax.rem(t + k, 8))

    def blk(k):
        return lax.rem(t + k, 8)

    def ring(r):
        return 2 * lax.rem(x + r // 2, 2) + lax.rem(c + r % 2, 2)

    counts = {"l": 0, "y": 0, "r": 0, "t": 0}
    pending = []
    left_already = []

    def leave(*copies):
        for copy in copies:
            copy.wait_send()
            left_already.append(copy)

    def local(src, dst):
        n = counts["l"]
        counts["l"] += 1
        copy = pltpu.make_async_copy(src, dst, lsem.at[n])
        copy.start()
        return copy

    def remote(kind, src, dst, device):
        sends, recvs = {
            "y": (ysend, yrecv),
            "r": (rowsend, rowrecv),
            "t": (tsend, trecv),
        }[kind]
        n = counts[kind]
        counts[kind] += 1
        copy = pltpu.make_async_remote_copy(
            src_ref=src,
            dst_ref=dst,
            send_sem=sends.at[n],
            recv_sem=recvs.at[n],
            device_id=device,
            device_id_type=MESH,
        )
        copy.start()
        pending.append(copy)
        return copy

    z = t // 2
    xh = t % 2

    def zpeer(k):
        return (s, 2 * lax.rem(z + k, 4) + xh)

    hpeer = (s, 2 * z + 1 - xh)
    load_tab = local(ctab_ref, tab.at[:, 0])
    load_chroma = local(chroma_ref, chroma)
    own_cols = pl.ds(pl.multiple_of(128 * t, 128), 128)
    dq_half = pl.ds(pl.multiple_of(512 * c, 512), 512)
    dq_part = pl.ds(pl.multiple_of(512 * c + 128 * y, 128), 128)
    dp_half = pl.ds(pl.multiple_of(64 * c, 64), 64)
    di_half = pl.ds(pl.multiple_of(256 * c, 256), 256)
    di_part = pl.ds(pl.multiple_of(256 * c + 64 * y, 64), 64)

    def di_of(block):
        return din_ref.at[pl.ds(pl.multiple_of(512 * block + 256 * c + 64 * y, 64), 64)]

    load_di = local(di_of(t), di.at[di_part, own_cols])
    load_weights = [
        local(dqkv_ref.at[0:2, dq_part], dq.at[0:2, dq_part, own_cols]),
        local(dqkv_ref.at[2, dq_half], dq.at[2, dq_half, own_cols]),
        local(dproj_ref.at[dp_half], dp.at[t, c]),
    ]


    cpb[0] = jnp.concatenate(
        [codes_ref[...], chroma_ids_ref[...], songs_ref[...], jnp.zeros((6, FR), jnp.int32)], axis=0
    )

    barrier = pltpu.get_barrier_semaphore()
    greeted = [ypeer(k) for k in (1, 2, 3)] + [sib, xpeer] + [tpeer(k) for k in range(1, 8)]
    for device in greeted:
        pl.semaphore_signal(barrier, inc=1, device_id=device, device_id_type=MESH)
    def to_columns(k):
        columns = jnp.transpose(cpb[k].astype(F32))
        colt[k] = jnp.concatenate(
            [
                columns[OWN * o + HALF * h : OWN * o + HALF * (h + 1)]
                for h in range(2)
                for o in range(8)
            ],
            axis=0,
        )

    lane = iota((1, 256), 1)
    lane_q = 2 * lax.rem(x + lane // 128, 2) + lax.rem(c + (lane // 64) % 2, 2)
    entry_row = (256 * y + 64 * lane_q + lane % 64).astype(F32)
    def encode(k):
        to_columns(k)
        for b in range(8):
            hot[k, :, 256 * b : 256 * (b + 1)] = jnp.where(
                colt[k, :, b : b + 1] == entry_row, 1.0, 0.0
            ).astype(BF16)

    encode(0)
    load_chroma.wait()
    chroma_hot = jnp.where(
        colt[0, :, 8:9] == iota((1, 256), 1).astype(F32), 1.0, 0.0
    ).astype(BF16)
    emb[...] = dot(chroma_hot, chroma[...])

    for copy in load_weights:
        copy.wait()
    load_tab.wait()
    pl.semaphore_wait(barrier, len(greeted))

    starts = (0, 128, 256, 384, 512)
    chunk = lambda j: pl.ds(starts[j], starts[j + 1] - starts[j])
    code_copies = {k: remote("y", cpb.at[0], cpb.at[k], ypeer(k)) for k in (1, 3, 2)}
    tab_x = []

    def next_table():
        j = len(tab_x)
        if j:
            leave(tab_x[-1])
        tab_x.append(
            remote("r", tab.at[:, 0, :, chunk(j)], tab.at[:, 2, :, chunk(j)], xpeer)
        )

    next_table()
    tab_s = remote("r", tab.at[:, 0], tab.at[:, 1], sib)

    def weights_at(block):
        cols = pl.ds(pl.multiple_of(128 * block, 128), 128)
        return (dq.at[0:2, dq_part, cols], dq.at[2, dq_half, cols], dp.at[block, c])

    def send_weights(block, device, which=(0, 1, 2)):
        return [remote("t", weights_at(block)[n], weights_at(block)[n], device) for n in which]

    di_copies = [remote("t", di_of(blk(k)), di.at[di_part, own_cols], tpeer(k)) for k in range(1, 8)]
    weights_z = [send_weights(t, zpeer(k), (0, 2)) for k in (1, 3, 2)]
    load_dtab = local(dtab_ref, dtab)
    load_w = local(wqkv_ref, wv)
    next_table()
    for k in (1, 3, 2):
        code_copies[k].wait_recv()
        encode(k)
        if k == 3:
            next_table()
    tab_s.wait_recv()

    part_copies = {}
    tok_copies = {}

    def partial(j):
        cols = slice(starts[j], starts[j + 1])
        tab_x[j].wait_recv()
        forward = remote("r", tab.at[:, 2, :, chunk(j)], tab.at[:, 3, :, chunk(j)], sib)
        forward.wait_recv()
        table = tab[:, :, :, cols].reshape(2048, starts[j + 1] - starts[j])
        for k in (2, 1, 3, 0):
            part = dot(hot[k], table)
            if k == 0:
                emb[:, cols] += part
            else:
                psend[k, :, cols] = part.astype(BF16)
                part_copies[j, k] = remote(
                    "y", psend.at[k, :, chunk(j)], prec.at[4 - k, :, chunk(j)], ypeer(4 - k)
                )

    def send_tokens(h, j, slot):
        for k in (1, 3, 2):
            tok_copies[h, j, 2 * k + slot] = remote(
                "t", toks.at[slot, h, :, chunk(j)], toks.at[2 * k + slot, h, :, chunk(j)], zpeer(k)
            )

    def own(h, j):
        tok_copies[h, j, 1] = remote(
            "t", toks.at[0, h, :, chunk(j)], toks.at[1, h, :, chunk(j)], hpeer
        )
        send_tokens(h, j, 0)

    def relay(h, j):
        tok_copies[h, j, 1].wait_recv()
        send_tokens(h, j, 1)

    def settle(j):
        cols = slice(starts[j], starts[j + 1])
        for k in (1, 3, 2):
            part_copies[j, k].wait_recv()
        total = emb[:, cols]
        for k in (1, 2, 3):
            total = total + prec[k, :, cols].astype(F32)
        toks[0, :, :, cols] = total.astype(BF16).reshape(2, HR, -1)
        own(0, j)

    partial(0)
    next_table()
    partial(1)
    partial(2)
    settle(0)
    partial(3)
    settle(1)
    relay(0, 0)
    own(1, 0)
    mate = 2 * z + 1 - xh
    weights_x = send_weights(t, hpeer)
    settle(2)
    relay(0, 1)
    own(1, 1)
    settle(3)
    relay(0, 2)
    relay(1, 0)
    relay(0, 3)
    relay(1, 1)
    own(1, 2)
    own(1, 3)
    relay(1, 2)
    relay(1, 3)

    load_di.wait()
    for copy in di_copies:
        copy.wait_recv()
    di_y = [remote("y", di.at[di_part], di.at[di_part], ypeer(k)) for k in (1, 3, 2)]

    load_dtab.wait()
    entry = iota((1, 1024), 1).astype(F32)
    for b in range(7):
        onehot = jnp.where(colt[0, :, b : b + 1] == entry, 1.0, 0.0).astype(BF16)
        lk[b] = dot(onehot, dtab[b]).astype(BF16).reshape(2, HR, 128)
    lkf[:, :, :, own_cols] = lk[:, :, pl.ds(pl.multiple_of(HALF * t, HALF), HALF)]

    base_cos = bases_ref[0, pl.ds(s, 1), :]
    base_sin = bases_ref[1, pl.ds(s, 1), :]
    song_lanes = jnp.transpose(colt[0])[9:10, :]
    song_row = iota((16, HEAD), 0)

    def project(h):
        ssq = jnp.zeros((HR, 1), F32)
        for n, slot in enumerate((0, 1, 2, 6, 4, 3, 7, 5)):
            if slot:
                for j in range(4):
                    if slot > 1:
                        tok_copies[h, j, slot].wait_recv()
            feature = 2 * lax.rem(z + 4 - slot // 2, 4) + lax.rem(xh + slot % 2, 2)
            block = toks[slot, h].astype(F32)
            ssq = ssq + jnp.sum(block * block, axis=1, keepdims=True)
            place = pl.ds(pl.multiple_of(512 * feature, 512), 512)
            scaled = (block * again_ref[:, place]).astype(BF16)
            for i in range(3):
                product = dot(scaled, wv[i, place, :])
                if n == 0:
                    acc[i] = product
                else:
                    acc[i] += product
        factor = lax.rsqrt(ssq * (1.0 / 4096) + 1e-05)
        rows = slice(HR * h, HR * (h + 1))
        cosines = rows_ref[0, rows] * base_cos - rows_ref[1, rows] * base_sin
        sines = rows_ref[1, rows] * base_cos + rows_ref[0, rows] * base_sin
        sines = jnp.where(iota((1, HEAD), 1) < 64, -sines, sines)
        song_rows = jnp.where(song_row == 0, song_lanes[:, rows], 0.0).astype(BF16)
        for g in range(4):
            cols = slice(HEAD * g, HEAD * (g + 1))
            for i, start in ((0, 2 * HR + 16), (1, 0), (2, HR)):
                entries = acc[i, :, cols] * factor
                if i < 2:
                    entries = entries * cosines + pltpu.roll(entries, 64, 1) * sines
                kvs[h, g, start : start + HR, :] = entries.astype(BF16)
            kvs[h, g, 2 * HR : 2 * HR + 16, :] = song_rows

    kv_copies = {}
    kv_x = {}
    kv_s = {}
    kv_f = {}
    shared = pl.ds(0, 2 * HR + 16)

    def over_y(h):
        for k in (1, 3, 2):
            kv_copies[h, k] = remote(
                "y", kvs.at[h, lax.rem(y + k, 4)], kvb.at[h, 0, k], ypeer(k)
            )
        kvb[h, 0, 0] = kvs[h, y]

    def over_row(h):
        for k in (0, 1, 3, 2):
            if k:
                kv_copies[h, k].wait_recv()
            kv_x[h, k] = remote("r", kvb.at[h, 0, k, shared], kvb.at[h, 2, k, shared], xpeer)
            kv_s[h, k] = remote("r", kvb.at[h, 0, k, shared], kvb.at[h, 1, k, shared], sib)

    def over_cores(h):
        for k in (0, 1, 3, 2):
            kv_x[h, k].wait_recv()
            kv_f[h, k] = remote("r", kvb.at[h, 2, k, shared], kvb.at[h, 3, k, shared], sib)

    load_w.wait()
    project(0)
    over_y(0)
    over_row(0)
    project(1)
    over_y(1)

    for copy in weights_x:
        copy.wait_recv()
    weights_zq = [send_weights(mate, zpeer(k), (0,)) for k in (1, 3, 2)]
    weights_zx = [send_weights(mate, zpeer(k), (1, 2)) for k in (1, 3, 2)]
    weights_zv = [send_weights(t, zpeer(k), (1,)) for k in (1, 3, 2)]
    load_wout = [
        local(wout_ref.at[:, pl.ds(512 * j, 512)], wv.at[0, pl.ds(512 * j, 512)]) for j in range(8)
    ]
    over_cores(0)
    over_row(1)

    lk_copies = [
        remote(
            "t",
            lk.at[:, :, pl.ds(pl.multiple_of(HALF * blk(k), HALF), HALF)],
            lkf.at[:, :, :, own_cols],
            tpeer(k),
        )
        for k in range(1, 8)
    ]

    for copies in weights_z + weights_zq:
        for copy in copies:
            copy.wait_recv()
    dq_y = [remote("y", dq.at[0:2, dq_part], dq.at[0:2, dq_part], ypeer(k)) for k in (1, 3, 2)]

    over_cores(1)
    for h in range(2):
        for k in (0, 1, 3, 2):
            kv_s[h, k].wait_recv()
            kv_f[h, k].wait_recv()

    scale = HEAD**-0.5 * float(np.log2(np.e))
    key_lane = iota((HR, FR), 1)
    query_row = iota((HR, FR), 0)
    behind = (
        OWN * ((key_lane % HR) // HALF) + HALF * (key_lane // HR) + key_lane % HALF
    ) - (OWN * (query_row // HALF) + query_row % HALF)
    head_cols = pl.ds(pl.multiple_of(HEAD * y, HEAD), HEAD)
    o_copies = {}

    def attend(half, kq):
        yq = lax.rem(y + 4 - kq, 4)
        earlier = jnp.minimum(yq, 2)
        queries = kvb[half, 0, kq, 2 * HR + 16 :, :]
        query_song = jnp.broadcast_to(
            colt[kq, HR * half : HR * (half + 1), 9:10], (HR, HEAD)
        )

        def highest_of(group, highest, same_row):
            kk = lax.rem(kq + group, 4)
            for r in range(4):
                keys = jnp.concatenate([kvb[0, r, kk, :HR, :], kvb[1, r, kk, :HR, :]], axis=0)
                found = lax.dot_general(
                    queries, keys, (((1,), (1,)), ((), ())), preferred_element_type=F32
                )
                songs = [kvb[h, r, kk, 2 * HR : 2 * HR + 16, :].astype(F32)[0:1] for h in range(2)]
                allowed = jnp.concatenate([query_song == song for song in songs], axis=1)
                if same_row:
                    allowed = allowed & (behind <= FR * (q4 - ring(r)) + HALF * half)
                found = jnp.where(allowed, found, -1e30)
                sbuf[4 * group + r] = found
                highest = jnp.maximum(highest, jnp.maximum(found[:, :HEAD], found[:, HEAD:]))
            return highest

        highest = highest_of(0, jnp.full((HR, HEAD), -1e30, F32), True)
        highest = lax.fori_loop(
            1, earlier + 1, lambda group, carry: highest_of(group, carry, False), highest
        )
        peak = jnp.max(highest, axis=1, keepdims=True) * scale

        def blend(group, carry):
            totals, blended = carry
            kk = lax.rem(kq + group, 4)
            for r in range(4):
                weights = jnp.exp2(sbuf[4 * group + r] * scale - peak)
                totals = totals + (weights[:, :HEAD] + weights[:, HEAD:])
                held = jnp.concatenate(
                    [kvb[0, r, kk, HR : 2 * HR, :], kvb[1, r, kk, HR : 2 * HR, :]], axis=0
                )
                blended = blended + dot(weights.astype(BF16), held)
            return totals, blended

        totals, blended = lax.fori_loop(
            0, earlier + 1, blend, (jnp.zeros((HR, HEAD), F32), jnp.zeros((HR, HEAD), F32))
        )
        result = (blended / jnp.sum(totals, axis=1, keepdims=True)).astype(BF16)
        if kq:
            ob[half, kq] = result
            o_copies[half, kq] = remote(
                "y", ob.at[half, kq], att.at[half, :, head_cols], ypeer(4 - kq)
            )
        else:
            att[half, :, head_cols] = result

    for half in range(2):
        for kq in (2, 1, 3, 0):
            attend(half, kq)

    for copy in load_wout:
        copy.wait()
    r_copies = {}

    def columns_of(k, d):
        block = 2 * lax.rem(z + k, 4) + lax.rem(xh + d, 2)
        return wv[0, pl.ds(pl.multiple_of(512 * block, 512), 512), :]

    def send_sum(h, slot, value, device):
        rsend[h, slot] = value.astype(BF16)
        r_copies[h, slot] = remote("t", rsend.at[h, slot], rrec.at[h, slot], device)

    def arrived(h, slot):
        r_copies[h, slot].wait_recv()
        return rrec[h, slot].astype(F32)

    for k in (1, 2, 3):
        o_copies[0, k].wait_recv()
    for k in (2, 1, 3, 0):
        send_sum(0, k, dot(att[0], columns_of(k, 1)), hpeer)
    for k in (1, 2, 3):
        o_copies[1, k].wait_recv()
    for d in (1, 0):
        for k in (2, 1, 3):
            send_sum(1, 2 * k + d, dot(att[1], columns_of(k, d)), zpeer(k))
        if d:
            leave(*[r_copies[1, 2 * k + 1] for k in (2, 1, 3)])
    passed = dot(att[1], columns_of(0, 1))
    for k in (1, 3, 2):
        passed = passed + arrived(1, 2 * k + 1)
    send_sum(1, 1, passed, hpeer)
    for k in (2, 1, 3):
        send_sum(0, 4 + k, dot(att[0], columns_of(k, 0)) + arrived(0, k), zpeer(k))
    for h in range(2):
        resid[h] = toks[0, h].astype(F32) + dot(att[h], columns_of(0, 0))

    for copies in weights_zx + weights_zv:
        for copy in copies:
            copy.wait_recv()
    for copy in di_y:
        copy.wait_recv()
    di_forward = remote("r", di.at[di_half], di.at[di_half], sib)
    dv_forward = remote("r", dq.at[2, dq_half], dq.at[2, dq_half], sib)
    dp_forward = remote("r", dp.at[:, c], dp.at[:, c], sib)

    p_copies = {}
    th_copies = []
    place = iota((HR, HEAD), 1)

    def hand_over(h):
        total = resid[h]
        for slot in (2, 4, 6, 1) if h else (0, 5, 7, 6):
            total = total + arrived(h, slot)
        thl[h] = total.astype(BF16)
        hidden = thl[h].astype(F32)
        square = jnp.sum(hidden * hidden, axis=1, keepdims=True)
        high = square.astype(BF16).astype(F32)
        middle = (square - high).astype(BF16).astype(F32)
        low = square - high - middle
        squares = jnp.where(
            place == 0, high, jnp.where(place == 1, middle, jnp.where(place == 2, low, 0.0))
        )
        pfull[h, :, :, 1024:] = squares.astype(BF16).reshape(8, HALF, HEAD)
        gain = ogain_ref[:, pl.ds(pl.multiple_of(512 * t, 512), 512)]
        scaled = (hidden * gain).astype(BF16)
        if h:
            di_forward.wait_recv()
        pfull[h, :, :, :1024] = dot(scaled, di[...]).astype(BF16).reshape(8, HALF, 1024)
        for k in range(1, 8):
            p_copies[h, k] = remote("t", pfull.at[h, blk(k)], prb.at[h, k], tpeer(k))
        thb[h, :, pl.ds(pl.multiple_of(512 * t, 512), 512)] = thl[
            h, pl.ds(pl.multiple_of(HALF * t, HALF), HALF), :
        ]

    hand_over(1)
    hand_over(0)
    leave(*[p_copies[0, k] for k in range(1, 8)])
    for h in range(2):
        for k in range(1, 8):
            th_copies.append(
                remote(
                    "t",
                    thl.at[h, pl.ds(pl.multiple_of(HALF * blk(k), HALF), HALF)],
                    thb.at[h, :, pl.ds(pl.multiple_of(512 * t, 512), 512)],
                    tpeer(k),
                )
            )
    for copy in dq_y:
        copy.wait_recv()
    dq_forward = remote("r", dq.at[0:2, dq_half], dq.at[0:2, dq_half], sib)
    for copy in lk_copies:
        copy.wait_recv()

    left = iota((1, 128), 1) < DHEAD
    seen_row = iota((256, 128), 0) % 128
    seen_col = iota((256, 128), 1)
    seen = (seen_col <= seen_row) & (seen_col >= (seen_row // 8) * 8)
    out_row = iota((HR, HR), 0)
    order = jnp.where(
        iota((HR, HR), 1) == (out_row % 8) * HALF + out_row // 8, 1.0, 0.0
    ).astype(BF16)
    zero = jnp.zeros((), BF16)

    def depth(h):
        summed = pfull[h, t].astype(F32)
        for k in range(1, 8):
            p_copies[h, k].wait_recv()
            summed = summed + prb[h, k].astype(F32)
        square = jnp.sum(summed[:, 1024:], axis=1, keepdims=True)
        projected = summed[:, :1024] * lax.rsqrt(square * (1.0 / 4096) + 1e-05)
        inputs = [projected.astype(BF16)]
        for b in range(7):
            inputs.append((projected + lkf[b, h].astype(F32)).astype(BF16))
        inputs = dot(order, jnp.concatenate(inputs, axis=0))
        factor = lax.rsqrt(jnp.mean(inputs * inputs, axis=1, keepdims=True) + 1e-05)
        normed = (inputs * factor * dgain_ref[...]).astype(BF16)
        projections = []
        for i in range(3):
            if h and i != 1:
                (dq_forward if i == 0 else dv_forward).wait_recv()
            projections.append(dot(normed, dq[i]).astype(BF16))
        depth_q, depth_k, depth_v = projections
        for p in range(8):
            cols = slice(128 * p, 128 * (p + 1))
            pair = depth_q[:, cols]
            both = jnp.concatenate(
                [jnp.where(left, pair, zero), jnp.where(left, zero, pair)], axis=0
            )
            found = lax.dot_general(
                both, depth_k[:, cols], (((1,), (1,)), ((), ())), preferred_element_type=F32
            )
            found = jnp.where(seen, found, -1e30)
            peak = jnp.max(found, axis=1, keepdims=True)
            weights = jnp.exp((found - peak) * DHEAD**-0.5)
            totals = jnp.sum(weights, axis=1, keepdims=True)
            blended = dot(weights.astype(BF16), depth_v[:, cols]) / totals
            mixed[:, cols] = jnp.where(left, blended[:128], blended[128:]).astype(BF16)
        if h:
            dp_forward.wait_recv()
        dh_out[HR * h : HR * (h + 1), :] = (
            inputs + dot(mixed[...], dp[...].reshape(1024, 1024))
        ).astype(BF16)

    depth(1)
    depth(0)
    for copy in th_copies:
        copy.wait_recv()
    th_out[...] = thb[...].reshape(OWN, 4096)
    for copy in pending:
        if not any(copy is other for other in left_already):
            copy.wait_send()


def shards(
    audio_codes,
    chroma_ids,
    song_ids,
    code_table,
    chroma_table,
    attention_gain,
    temporal_qkv,
    temporal_out,
    output_gain,
    depth_input,
    depth_table,
    depth_gain,
    depth_qkv,
    depth_proj,
):
    rows, bases = rotation_tables()
    vmem = pl.BlockSpec(memory_space=pltpu.VMEM)
    anywhere = pl.BlockSpec(memory_space=pl.ANY)
    temporal, depth = pl.pallas_call(
        kernel,
        out_shape=(
            jax.ShapeDtypeStruct((OWN, 4096), BF16),
            jax.ShapeDtypeStruct((FR, 1024), BF16),
        ),
        in_specs=[vmem] * 8 + [anywhere] * 8,
        out_specs=(vmem, vmem),
        scratch_shapes=[
            pltpu.VMEM((3, 4096, 512), BF16),
            pltpu.VMEM((8, 4, 64, 512), BF16),
            pltpu.VMEM((4, FR, 2048), BF16),
            pltpu.VMEM((256, 512), BF16),
            pltpu.VMEM((7, 1024, 128), BF16),
            pltpu.VMEM((7, 2, HR, 128), BF16),
            pltpu.VMEM((7, 2, HALF, 1024), BF16),
            pltpu.VMEM((4, 16, FR), jnp.int32),
            pltpu.VMEM((4, FR, 16), F32),
            pltpu.VMEM((FR, 512), F32),
            pltpu.VMEM((2, HR, 512), F32),
            pltpu.VMEM((4, FR, 512), BF16),
            pltpu.VMEM((4, FR, 512), BF16),
            pltpu.VMEM((8, 2, HR, 512), BF16),
            pltpu.VMEM((3, HR, 512), F32),
            pltpu.VMEM((2, 4, PIECE, HEAD), BF16),
            pltpu.VMEM((2, 4, 4, PIECE, HEAD), BF16),
            pltpu.VMEM((12, HR, FR), F32),
            pltpu.VMEM((2, 4, HR, HEAD), BF16),
            pltpu.VMEM((2, HR, 512), BF16),
            pltpu.VMEM((2, 8, HR, 512), BF16),
            pltpu.VMEM((2, 8, HR, 512), BF16),
            pltpu.VMEM((2, HR, 512), BF16),
            pltpu.VMEM((2, HALF, 4096), BF16),
            pltpu.VMEM((512, 1024), BF16),
            pltpu.VMEM((2, 8, HALF, 1152), BF16),
            pltpu.VMEM((2, 8, HALF, 1152), BF16),
            pltpu.VMEM((3, 1024, 1024), BF16),
            pltpu.VMEM((8, 2, 64, 1024), BF16),
            pltpu.VMEM((HR, 1024), BF16),
            pltpu.SemaphoreType.DMA((16,)),
            pltpu.SemaphoreType.DMA((33,)),
            pltpu.SemaphoreType.DMA((33,)),
            pltpu.SemaphoreType.DMA((37,)),
            pltpu.SemaphoreType.DMA((37,)),
            pltpu.SemaphoreType.DMA((133,)),
            pltpu.SemaphoreType.DMA((133,)),
        ],
        compiler_params=pltpu.CompilerParams(
            collective_id=0, has_side_effects=True, vmem_limit_bytes=60 * 1024 * 1024
        ),
        name="layer",
    )(
        audio_codes.T,
        chroma_ids[None],
        song_ids[None],
        attention_gain[None],
        output_gain[None],
        depth_gain[None],
        rows,
        bases,
        code_table,
        chroma_table,
        temporal_qkv,
        temporal_out,
        depth_input,
        depth_table,
        depth_qkv,
        depth_proj,
    )
    return temporal, depth.reshape(OWN, 8, 1024)


def solution(mesh):
    placed = (
        P("seq", None),
        P("seq"),
        P("seq"),
        P(None, "seq", "tensor"),
        P(None, "tensor"),
        P(),
        P(None, None, "tensor"),
        P("tensor", None),
        P(),
        P(None, "tensor"),
        P(None, None, "tensor"),
        P(),
        P(None, None, "tensor"),
        P("tensor", None),
    )
    return jax.shard_map(
        shards,
        mesh=mesh,
        in_specs=placed,
        out_specs=(P(("seq", "tensor"), None), P(("seq", "tensor"), None, None)),
        check_vma=False,
    )
```

time: 139 us -> 133 us (0.957); the launches traced: 139 us -> 131 us
  Pallas kernels: 134 us -> 127 us
    pallas_call x1, Pallas kernels: 134 us -> 127 us  [shards(): pl.pallas_call(kernel, out_shape=(jax.ShapeDtypeStruct((OWN, 4096), BF16)...]
where the time goes in v3:
time: 133 us; the launch traced here: 131 us
  Pallas kernels  127 us (95%)
  local copies, waits for them, and re-layouts  3.54 us (3%)
    pallas_call x1, Pallas kernels, shards(): pl.pallas_call(kernel, out_shape=(jax.ShapeDtypeStruct((OWN, 4096), BF16)...  127 us
    unnamed x2, local copies, waits for them, and re-layouts  3.54 us

profile of v3, /device:TPU:1, one launch (start us, length us, event | category | flops | bytes accessed | tf_op | source)
XLA Modules:
  0.0 130.9 jit_solution(12475106081929921100)
XLA Ops:
  0.6 126.7 %layer.1 = (bf16[32,4096]{1,0:T(8,128)(2,1)}, bf16[256,1024]{1,0:T(8,128)(2,1)}) custom-call(s32[8,256]{1,0:T(8,128)} %bitcast.10, s32[1,256]{1,0:T(1,128)} %bitcast.12, s32[1,256]{1,0:T(1,128)} %bitcast.13, f32[1,4096]{1,0:T(1,128)} %bitcast.8, f32[1,4096]{1,0:T(1,128)} %bitcast.9, f32[1,1024]{1,0:T(1,128)} %bitcast.11, ...), custom_call_target="tpu_custom_call" | custom-call | tf_op jit(solution)/shard_map/layer/pallas_call | solution.py:682
  127.4 1.7 %copy.20 = bf16[32,4096]{1,0:T(8,128)(2,1)} copy(bf16[32,4096]{1,0:T(8,128)(2,1)} %get-tuple-element.8) | data formatting | bytes 524288
  129.1 1.9 %copy.21 = bf16[32,8,1024]{2,1,0:T(8,128)(2,1)} copy(bf16[32,8,1024]{2,1,0:T(8,128)(2,1)} %bitcast.7) | data formatting | bytes 1048576

commit v4 on v3

--- a/solution.py
+++ b/solution.py
@@ -429,12 +429,13 @@
         for k in range(1, 8)
     ]
 
+    over_cores(1)
+
     for copies in weights_z + weights_zq:
         for copy in copies:
             copy.wait_recv()
     dq_y = [remote("y", dq.at[0:2, dq_part], dq.at[0:2, dq_part], ypeer(k)) for k in (1, 3, 2)]
 
-    over_cores(1)
     for h in range(2):
         for k in (0, 1, 3, 2):
             kv_s[h, k].wait_recv()
@@ -583,6 +584,9 @@
 
     hand_over(1)
     hand_over(0)
+    for copy in dq_y:
+        copy.wait_recv()
+    dq_forward = remote("r", dq.at[0:2, dq_half], dq.at[0:2, dq_half], sib)
     leave(*[p_copies[0, k] for k in range(1, 8)])
     for h in range(2):
         for k in range(1, 8):
@@ -594,9 +598,6 @@
                     tpeer(k),
                 )
             )
-    for copy in dq_y:
-        copy.wait_recv()
-    dq_forward = remote("r", dq.at[0:2, dq_half], dq.at[0:2, dq_half], sib)
     for copy in lk_copies:
         copy.wait_recv()
 

time: 133 us -> 131 us (0.985); the launches traced: 131 us -> 130 us
  no operation moved by 1% of the time
where the time goes in v4:
time: 131 us; the launch traced here: 130 us
  Pallas kernels  126 us (96%)
  local copies, waits for them, and re-layouts  3.54 us (3%)
    pallas_call x1, Pallas kernels, shards(): pl.pallas_call(kernel, out_shape=(jax.ShapeDtypeStruct((OWN, 4096), BF16)...  126 us
    unnamed x2, local copies, waits for them, and re-layouts  3.54 us

profile of v4, /device:TPU:1, one launch (start us, length us, event | category | flops | bytes accessed | tf_op | source)
XLA Modules:
  0.0 130.3 jit_solution(4651365878655655539)
XLA Ops:
  0.6 126.1 %layer.1 = (bf16[32,4096]{1,0:T(8,128)(2,1)}, bf16[256,1024]{1,0:T(8,128)(2,1)}) custom-call(s32[8,256]{1,0:T(8,128)} %bitcast.10, s32[1,256]{1,0:T(1,128)} %bitcast.12, s32[1,256]{1,0:T(1,128)} %bitcast.13, f32[1,4096]{1,0:T(1,128)} %bitcast.8, f32[1,4096]{1,0:T(1,128)} %bitcast.9, f32[1,1024]{1,0:T(1,128)} %bitcast.11, ...), custom_call_target="tpu_custom_call" | custom-call | tf_op jit(solution)/shard_map/layer/pallas_call | solution.py:683
  126.8 1.7 %copy.20 = bf16[32,4096]{1,0:T(8,128)(2,1)} copy(bf16[32,4096]{1,0:T(8,128)(2,1)} %get-tuple-element.8) | data formatting | bytes 524288
  128.5 1.9 %copy.21 = bf16[32,8,1024]{2,1,0:T(8,128)(2,1)} copy(bf16[32,8,1024]{2,1,0:T(8,128)(2,1)} %bitcast.7) | data formatting | bytes 1048576
